TPU v7x, 32 devices: a whole 2x2x4 slice. The times are simulated.
32 devices in a mesh: lat: 2 (over core), lev: 16 (over z, y, x).
Axes of the slice: x: 2, y: 2, z: 4, core: 2. Of those that a mesh axis runs over, the one named last changes fastest.
Arguments:
- field: float32 [32, 8, 128, 1152], P('lev', None, 'lat'), may hold values from 0.05 to 5
- courant: float32 [3, 32, 128, 1152], P(None, 'lev', 'lat'), may hold values from 0.02 to 0.3
- parcel_mass: float32 [8, 131072], P(None, ('lat', 'lev')), may hold values from 0.5 to 20
- parcel_owner: int32 [131072, 1], P(('lat', 'lev')), may hold values from 0 to 31; in each aligned block of 4096 rows (0 to 4095, 4096 to 8191, ...) at most 256 rows name the same one
- parcel_cell: int32 [131072], P(('lat', 'lev')), may hold values from 0 to 147455
- settle: float32 [8, 32], replicated, may hold values from 0.3 to 8
- coag_gain: float32 [8, 8, 8], replicated, may hold values from 0.002 to 0.03
- coag_loss: float32 [8, 8], replicated, may hold values from 0.02 to 0.5
Outputs:
- result: float32 [32, 8, 128, 1152], P('lev', None, 'lat')
Inputs may be any that keep to these rules, and one draw needn't show every extreme that they name: `parcel_owner`: among the parcels of one device, at most 256 have the same owner, and in some devices exactly 256 do.
All inputs are finite; a program needn't handle non-finite values.
Results may differ from a plain program's by a relative error of at most 0.0003.
Values sent between devices are 32-bit elements; how exact they have to be, the bound alone decides.
No kernel may reach another device: no remote copies, remote signals or barrier semaphores. Data moves between devices by JAX's collectives and lax.ppermute only.
A program may use at most 192 MiB of HBM per device.

v0:
```python
import functools

import jax
import jax.numpy as jnp
from jax import lax
from jax.experimental import pallas as pl
from jax.experimental.pallas import tpu as pltpu
from jax.sharding import PartitionSpec as P

ADV_STEPS = 2
LANES = 128
ROUTE_BLOCK = 256
ACCS = 4
UNROLL = 8
VMEM = pl.BlockSpec(memory_space=pltpu.VMEM)
SMEM = pl.BlockSpec(memory_space=pltpu.SMEM)
BIG = pltpu.CompilerParams(vmem_limit_bytes=56 * 1024 * 1024)


def route_kernel(devices, cap_lanes, level_cells, owner_ref, cell_ref, mass_ref, out_ref, a_ref, c_ref, b_ref):
    parcels = owner_ref.shape[1]
    blocks = cap_lanes // LANES
    width = ROUTE_BLOCK
    dev_ids = lax.broadcasted_iota(jnp.int32, (devices, width), 0)
    before = (
        lax.broadcasted_iota(jnp.int32, (width, width), 0) < lax.broadcasted_iota(jnp.int32, (width, width), 1)
    ).astype(jnp.bfloat16)
    slot_ids = lax.broadcasted_iota(jnp.int32, (cap_lanes, width), 0)

    def masks(start):
        owner = owner_ref[:, pl.ds(start, width)]
        cell = cell_ref[:, pl.ds(start, width)]
        mine = owner == dev_ids
        low = cell >= level_cells
        return owner, cell, jnp.where(mine & low, 1.0, 0.0), jnp.where(mine & (~low), 1.0, 0.0)

    low_total = jnp.zeros((devices, 1), jnp.float32)
    for start in range(0, parcels, width):
        unused, unused, low, high = masks(start)
        low_total = low_total + jnp.sum(low, axis=1, keepdims=True)
    low_base = jnp.zeros((devices, 1), jnp.float32)
    high_base = low_total
    for start in range(0, parcels, width):
        owner, cell, low, high = masks(start)
        both = jnp.concatenate([low, high], axis=0)
        earlier = jnp.dot(both.astype(jnp.bfloat16), before, preferred_element_type=jnp.float32)
        rank = jnp.sum(both * (earlier + jnp.concatenate([low_base, high_base], axis=0)), axis=0, keepdims=True)
        low_base = low_base + jnp.sum(low, axis=1, keepdims=True)
        high_base = high_base + jnp.sum(high, axis=1, keepdims=True)
        b_ref[:, pl.ds(start, width)] = jnp.where(slot_ids == rank.astype(jnp.int32), 1.0, 0.0).astype(jnp.bfloat16)
        mass = mass_ref[:, pl.ds(start, width)]
        coarse = mass.astype(jnp.bfloat16).astype(jnp.float32)
        fine = mass - coarse
        owner_rows = jnp.broadcast_to(owner, (8, width))
        for device in range(0, devices, 2):
            for part, piece in enumerate((coarse, fine)):
                pair = jnp.concatenate(
                    [jnp.where(owner_rows == device + extra, piece, 0.0) for extra in range(2)], axis=0
                )
                a_ref[pl.ds(part * devices * 8 + device * 8, 16), pl.ds(start, width)] = pair.astype(jnp.bfloat16)
        mine = low + high
        for part, piece in enumerate((cell >> 16, (cell >> 8) & 255, cell & 255)):
            c_ref[pl.ds(part * devices, devices), pl.ds(start, width)] = (mine * piece.astype(jnp.float32)).astype(
                jnp.bfloat16
            )
    contract = (((1,), (1,)), ((), ()))
    sorted_mass = lax.dot_general(a_ref[...], b_ref[...], contract, preferred_element_type=jnp.float32)
    sorted_cell = lax.dot_general(c_ref[...], b_ref[...], contract, preferred_element_type=jnp.float32)
    code = (
        sorted_cell[:devices] * 65536.0 + sorted_cell[devices : 2 * devices] * 256.0 + sorted_cell[2 * devices :]
    )
    total = sorted_mass[: devices * 8] + sorted_mass[devices * 8 :]
    out_ref[:, :, pl.ds(0, cap_lanes)] = total.reshape(devices, 8, cap_lanes)
    rows = lax.broadcasted_iota(jnp.int32, (8, LANES), 0)
    for device in range(devices):
        tile = jnp.zeros((8, LANES), jnp.float32)
        for block in range(blocks):
            tile = jnp.where(rows == block, code[device : device + 1, block * LANES : (block + 1) * LANES], tile)
        tile = jnp.where(rows == blocks, high_base[device : device + 1], tile)
        tile = jnp.where(rows == blocks + 1, low_base[device : device + 1], tile)
        out_ref[device, :, pl.ds(cap_lanes, LANES)] = tile


def route(parcel_mass, parcel_owner, parcel_cell, devices, level_cells):
    parcels = parcel_owner.shape[0]
    capacity = 2 * parcels // devices
    cap_lanes = -(-capacity // LANES) * LANES
    return pl.pallas_call(
        functools.partial(route_kernel, devices, cap_lanes, level_cells),
        out_shape=jax.ShapeDtypeStruct((devices, 8, cap_lanes + LANES), jnp.float32),
        in_specs=[VMEM] * 3,
        out_specs=VMEM,
        scratch_shapes=[
            pltpu.VMEM((devices * 16, parcels), jnp.bfloat16),
            pltpu.VMEM((devices * 3, parcels), jnp.bfloat16),
            pltpu.VMEM((cap_lanes, parcels), jnp.bfloat16),
        ],
        compiler_params=BIG,
        name="route",
    )(parcel_owner.reshape(1, parcels), parcel_cell.reshape(1, parcels), parcel_mass)


def deposit_kernel(row_offset, counts_ref, codes_ref, slots_ref, field_ref, out_ref, *accs):
    sources, unused, width = slots_ref.shape
    cap_lanes = width - LANES
    levels, bins, lats, lons = field_ref.shape
    lon_blocks = lons // LANES
    rows = levels * lats * lon_blocks
    lane_ids = lax.broadcasted_iota(jnp.int32, (8, LANES), 1)

    def clear(index, carry):
        for acc in accs:
            acc[pl.ds(index * 8, 8)] = jnp.zeros((8, 8, LANES), jnp.float32)
        return carry

    lax.fori_loop(0, rows // 8, clear, 0)

    def from_source(source, carry):
        def chunk(index, carry):
            first = index * UNROLL
            block = first // LANES
            masses = slots_ref[source, :, pl.ds(pl.multiple_of(block * LANES, LANES), LANES)]
            base = source * cap_lanes + first
            for step in range(UNROLL):
                code = codes_ref[base + step]
                row = (code >> 7) - row_offset
                if row_offset:
                    row = jnp.where(row < 0, rows, row)
                lane = code & (LANES - 1)
                moved = pltpu.roll(masses, (lane - first - step) & (LANES - 1), 1)
                acc = accs[step % ACCS]
                acc[row] = acc[row] + jnp.where(lane_ids == lane, moved, 0.0)
            return carry

        return lax.fori_loop(0, (counts_ref[source] + UNROLL - 1) // UNROLL, chunk, carry)

    lax.fori_loop(0, sources, from_source, 0)

    flat = [acc.reshape((rows + 8) * 8, LANES) for acc in accs]

    def merge(index, carry):
        level = index // (lats // 8)
        lat = (index % (lats // 8)) * 8
        for lon in range(lon_blocks):
            for b in range(bins):
                start = ((level * lats + lat) * lon_blocks + lon) * 8 + b
                picked = pl.ds(start, 8, stride=lon_blocks * 8)
                total = field_ref[level, b, pl.ds(pl.multiple_of(lat, 8), 8), pl.ds(lon * LANES, LANES)]
                for acc in flat:
                    total = total + acc[picked, :]
                out_ref[level, b, pl.ds(pl.multiple_of(lat, 8), 8), pl.ds(lon * LANES, LANES)] = total
        return carry

    lax.fori_loop(0, levels * (lats // 8), merge, 0)


def deposit(field, slots, codes, counts, row_offset, name):
    levels, bins, lats, lons = field.shape
    rows = levels * lats * lons // LANES
    return pl.pallas_call(
        functools.partial(deposit_kernel, row_offset),
        out_shape=jax.ShapeDtypeStruct(field.shape, jnp.float32),
        in_specs=[SMEM, SMEM, VMEM, VMEM],
        out_specs=VMEM,
        scratch_shapes=[pltpu.VMEM((rows + 8, 8, LANES), jnp.float32)] * ACCS,
        compiler_params=BIG,
        name=name,
    )(counts, codes, slots, field)


def advance_kernel(par_ref, f_ref, rim_ref, halo_ref, c_ref, ch_ref, cn_ref, adv_ref, hl_ref, p0, p1):
    step = pl.program_id(0)
    bins = f_ref.shape[1]

    @pl.when(step == 0)
    def halo():
        def one(b, carry):
            above = halo_ref[0, b]
            for level in range(2):
                f = halo_ref[1 + level, b]
                rolled = pltpu.roll(f, 1, 0)
                p0[level, b] = rolled
                new = (
                    f
                    - ch_ref[0, level] * (f - pltpu.roll(f, 1, 1))
                    - ch_ref[1, level] * (f - rolled)
                    - ch_ref[2, level] * (f - above)
                )
                p1[level, b] = pltpu.roll(new, 1, 0)
                above = f
            return carry

        lax.fori_loop(0, bins, one, 0)

    @pl.when(step > 0)
    def main():
        top_row = lax.broadcasted_iota(jnp.int32, f_ref.shape[2:], 0) == 0

        def south(prev, level, b, f):
            rolled = pltpu.roll(f, 1, 0)
            out = jnp.where(top_row, prev[level, b], rolled)
            prev[level, b] = rolled
            return out

        def one(b, carry):
            f0 = f_ref[0, b]
            f1 = f_ref[1, b]
            g0 = (
                f0
                - c_ref[0, 0] * (f0 - pltpu.roll(f0, 1, 1))
                - c_ref[1, 0] * (f0 - south(p0, 0, b, f0))
                - c_ref[2, 0] * (f0 - rim_ref[b])
            )
            g1 = (
                f1
                - c_ref[0, 1] * (f1 - pltpu.roll(f1, 1, 1))
                - c_ref[1, 1] * (f1 - south(p0, 1, b, f1))
                - c_ref[2, 1] * (f1 - f0)
            )
            a0 = (
                g0
                - c_ref[0, 0] * (g0 - pltpu.roll(g0, 1, 1))
                - c_ref[1, 0] * (g0 - south(p1, 0, b, g0))
                - c_ref[2, 0] * g0
            )
            a1 = (
                g1
                - c_ref[0, 1] * (g1 - pltpu.roll(g1, 1, 1))
                - c_ref[1, 1] * (g1 - south(p1, 1, b, g1))
                - c_ref[2, 1] * (g1 - g0)
            )
            adv_ref[0, b] = a0
            adv_ref[1, b] = a1
            low = (a1 + par_ref[b] * (a0 * par_ref[8 + b])) * par_ref[24 + b]
            hl_ref[0, b] = cn_ref[...] * g1 + par_ref[16 + b] * low
            return carry

        lax.fori_loop(0, bins, one, 0)


def advance(params, field, rim, halo, courant, courant_halo, courant_next):
    levels, bins, lats, lons = field.shape
    blocks = lats // 8
    at = lambda step: jnp.maximum(step - 1, 0)
    return pl.pallas_call(
        advance_kernel,
        out_shape=(
            jax.ShapeDtypeStruct(field.shape, jnp.float32),
            jax.ShapeDtypeStruct((blocks, bins, 8, lons), jnp.float32),
        ),
        grid=(blocks + 1,),
        in_specs=[
            SMEM,
            pl.BlockSpec((levels, bins, 8, lons), lambda step: (0, 0, at(step), 0)),
            pl.BlockSpec((bins, 8, lons), lambda step: (0, at(step), 0)),
            pl.BlockSpec((3, bins, 8, lons), lambda step: (0, 0, 0, 0)),
            pl.BlockSpec((3, levels, 8, lons), lambda step: (0, 0, at(step), 0)),
            pl.BlockSpec((3, levels, 8, lons), lambda step: (0, 0, 0, 0)),
            pl.BlockSpec((8, lons), lambda step: (at(step), 0)),
        ],
        out_specs=(
            pl.BlockSpec((levels, bins, 8, lons), lambda step: (0, 0, at(step), 0)),
            pl.BlockSpec((1, bins, 8, lons), lambda step: (at(step), 0, 0, 0)),
        ),
        scratch_shapes=[pltpu.VMEM((levels, bins, 8, lons), jnp.float32)] * 2,
        compiler_params=BIG,
        name="advance",
    )(params, field, rim, halo, courant, courant_halo, courant_next)


def cube_end_kernel(lam_ref, hl_ref, out_ref):
    count, bins = hl_ref.shape[:2]

    def one(b, carry):
        h = hl_ref[0, b]
        for member in range(1, count):
            h = hl_ref[member, b] + lam_ref[member * bins + b] * h
        out_ref[b] = h
        return carry

    lax.fori_loop(0, bins, one, 0)


def cube_scan_kernel(lam_ref, hl_ref, hin_ref, out_ref):
    count, bins = hl_ref.shape[:2]

    def one(b, carry):
        h = hin_ref[b]
        out_ref[0, b] = h
        for member in range(count - 1):
            h = hl_ref[member, b] + lam_ref[member * bins + b] * h
            out_ref[member + 1, b] = h
        return carry

    lax.fori_loop(0, bins, one, 0)


def finish_kernel(par_ref, loss_ref, gain_ref, adv_ref, h_ref, out_ref):
    levels, bins, unused, lons = adv_ref.shape
    width = 3 * LANES

    def part(index, carry):
        at = pl.ds(pl.multiple_of(index * width, LANES), width)
        above = [h_ref[0, b, :, at] for b in range(bins)]
        for level in range(2):
            solved = []
            for b in range(bins):
                s = (adv_ref[level, b, :, at] + above[b]) * par_ref[16 * level + 8 + b]
                solved.append(s)
                above[b] = par_ref[b] * s
            for i in range(bins):
                loss = loss_ref[i * bins] * solved[0]
                for j in range(1, bins):
                    loss = loss + loss_ref[i * bins + j] * solved[j]
                total = solved[i]
                base = i * bins * bins
                for j in range(bins):
                    inner = gain_ref[base + j * bins] * solved[0]
                    for k in range(1, j + 1):
                        inner = inner + gain_ref[base + j * bins + k] * solved[k]
                    total = total + inner * solved[j]
                out_ref[level, i, :, at] = total / (1.0 + loss)
        return carry

    lax.fori_loop(0, lons // width, part, 0)


def finish(params, loss, gain, adv, h):
    levels, bins, lats, lons = adv.shape
    return pl.pallas_call(
        finish_kernel,
        out_shape=jax.ShapeDtypeStruct(adv.shape, jnp.float32),
        grid=(lats // 8,),
        in_specs=[
            SMEM,
            SMEM,
            SMEM,
            pl.BlockSpec((levels, bins, 8, lons), lambda step: (0, 0, step, 0)),
            pl.BlockSpec((1, bins, 8, lons), lambda step: (step, 0, 0, 0)),
        ],
        out_specs=pl.BlockSpec((levels, bins, 8, lons), lambda step: (0, 0, step, 0)),
        compiler_params=BIG,
        name="finish",
    )(params, loss, gain, adv, h)


def shifted(value, axis, steps):
    count = lax.axis_size(axis)
    first, last = (max(0, -steps), min(count, count - steps))
    return lax.ppermute(value, axis, [(source, source + steps) for source in range(first, last)])


def on_device(field, courant, parcel_mass, parcel_owner, parcel_cell, settle, coag_gain, coag_loss):
    levels, bins, lats, lons = field.shape
    n_lev = lax.axis_size("lev")
    devices = lax.axis_size(("lat", "lev"))
    cube = lats // 8
    cubes = n_lev // cube
    here = lax.axis_index("lev")

    raw_rim = shifted(field[-1], "lev", 1)
    courant_next = shifted(courant[2, 0], "lev", -1)
    courant_halo = shifted(courant[:, :, -8:], "lat", 1)

    slots = route(parcel_mass, parcel_owner, parcel_cell, devices, lats * lons)
    slots = lax.all_to_all(slots, ("lat", "lev"), split_axis=0, concat_axis=0, tiled=True)
    cap_lanes = slots.shape[2] - LANES
    blocks = cap_lanes // LANES
    rim_slots = shifted(slots, "lev", 1)

    def tables(slots, row):
        codes = slots[:, :blocks, cap_lanes:].astype(jnp.int32).reshape(devices * cap_lanes)
        counts = slots[:, row, cap_lanes].astype(jnp.int32)
        return codes, counts

    codes, counts = tables(slots, blocks)
    f0 = deposit(field, slots, codes, counts, 0, "deposit")
    codes, counts = tables(rim_slots, blocks + 1)
    rim = deposit(raw_rim[None], rim_slots, codes, counts, lats * lons // LANES, "deposit_rim")[0]
    halo = shifted(jnp.concatenate([rim[None, :, -8:], f0[:, :, -8:]], axis=0), "lat", 1)

    pairs = settle.reshape(bins, n_lev, 2)
    first, second = pairs[:, :, 0], pairs[:, :, 1]
    table = jnp.stack([first, 1.0 / (1.0 + first), second, 1.0 / (1.0 + second)], axis=0)
    params = lax.dynamic_index_in_dim(table, here, axis=2, keepdims=False).reshape(4 * bins)
    lam = (table[0] * table[1] * table[2] * table[3]).T
    lam = lax.dynamic_slice_in_dim(lam, here // cube * cube, cube, axis=0)
    gain = coag_gain + jnp.swapaxes(coag_gain, 1, 2)
    gain = jnp.where(jnp.eye(bins, dtype=bool)[None], coag_gain, gain)

    adv, hl = advance(params, f0, rim, halo, courant, courant_halo, courant_next)

    groups = [list(range(c * cube, (c + 1) * cube)) for c in range(cubes)]
    swap = functools.partial(
        lax.all_to_all, axis_name="lev", split_axis=0, concat_axis=0, axis_index_groups=groups, tiled=True
    )
    hl = swap(hl)
    flat_lam = lam.reshape(cube * bins)
    end = pl.pallas_call(
        cube_end_kernel,
        out_shape=jax.ShapeDtypeStruct(hl.shape[1:], jnp.float32),
        in_specs=[SMEM, VMEM],
        out_specs=VMEM,
        compiler_params=BIG,
        name="cube_end",
    )(flat_lam, hl)
    reach = 1
    factor = jnp.prod(lam, axis=0)[:, None, None]
    while reach < cubes - 1:
        end = end + factor * shifted(end, "lev", reach * cube)
        factor = factor * shifted(factor, "lev", reach * cube)
        reach = 2 * reach
    carried = shifted(end, "lev", cube)
    h = pl.pallas_call(
        cube_scan_kernel,
        out_shape=jax.ShapeDtypeStruct(hl.shape, jnp.float32),
        in_specs=[SMEM, VMEM, VMEM],
        out_specs=VMEM,
        compiler_params=BIG,
        name="cube_scan",
    )(flat_lam, hl, carried)
    h = swap(h)
    return finish(params, coag_loss.reshape(-1), gain.reshape(-1), adv, h)


def solution(mesh):
    in_specs = (
        P("lev", None, "lat", None),
        P(None, "lev", "lat", None),
        P(None, ("lat", "lev")),
        P(("lat", "lev"), None),
        P(("lat", "lev")),
        P(),
        P(),
        P(),
    )
    out_specs = P("lev", None, "lat", None)
    return jax.shard_map(
        on_device, mesh=mesh, in_specs=in_specs, out_specs=out_specs, check_vma=False
    )
```

profile of v0, /device:TPU:0, one launch (start us, length us, event | category | flops | bytes accessed | tf_op | source)
XLA Modules:
  0.0 358.4 jit_solution(12031850633494387230)
XLA Ops:
  0.0 1.8 slice_bitcast_fusion
  1.8 5.0 %collective-permute-start.1 = (f32[8,64,1152]{2,1,0:T(8,128)S(1)}, f32[8,64,1152]{2,1,0:T(8,128)S(1)}, u32[]{:S(2)}, u32[]{:S(2)}) collective-permute-start(f32[8,64,1152]{2,1,0:T(8,128)S(1)} %slice_bitcast_fusion), channel_id=1, source_target_pairs={{0,1},{1,2},{2,3},{3,4},{4,5},{5,6},{6,7},{7,8},{8,9},{9,10},{10,1... | collective-permute-start | bytes 7077896 | tf_op jit(solution)/shard_map/ppermute | solution.py:350
  6.8 4.0 %route.1 = f32[32,8,384]{2,1,0:T(8,128)} custom-call(s32[1,4096]{1,0:T(1,128)} %bitcast.47, s32[1,4096]{1,0:T(1,128)} %bitcast.48, f32[8,4096]{1,0:T(8,128)} %mass_ref.1), custom_call_target="tpu_custom_call" | custom-call | tf_op jit(solution)/shard_map/route/pallas_call | solution.py:88
  10.8 52.7 %all_to_all.15.slots_ref = f32[32,8,384]{2,1,0:T(8,128)S(1)} all-to-all(f32[32,8,384]{2,1,0:T(8,128)} %route.1), channel_id=1, replica_groups=mesh['lat'=2,'lev'=16] {'lat','lev'}, dimensions={0} | all-to-all | bytes 786432 | tf_op jit(solution)/shard_map/all_to_all | solution.py:366
  63.5 0.0 copy-start.3
  63.5 3.2 collective-permute-start
  66.8 1.2 fusion.1.counts_ref
  67.9 0.6 slice_convert_fusion.1
  68.6 0.0 copy-done.3
  68.6 89.2 %deposit.1.f_ref = f32[2,8,64,1152]{3,2,1,0:T(8,128)} custom-call(s32[32]{0:T(128)} %fusion.1.counts_ref, s32[8192]{0:T(1024)} %bitcast.43, f32[32,8,384]{2,1,0:T(8,128)} %copy-done.3, f32[2,8,64,1152]{3,2,1,0:T(8,128)} %field_ref.1), custom_call_target="tpu_custom_call" | custom-call | tf_op jit(solution)/shard_map/deposit/pallas_call | solution.py:160
  157.7 0.0 collective-permute-done.slots_ref
  157.7 0.0 copy-start.5
  157.7 1.3 fusion.counts_ref
  159.0 0.6 slice_convert_fusion
  159.6 0.0 collective-permute-done.1
  159.6 0.0 copy-start.2
  159.6 0.0 copy-done.5
  159.6 1.4 copy-done.2
  161.0 0.0 slice-start
  161.0 6.3 %deposit_rim.1 = f32[1,8,64,1152]{3,2,1,0:T(8,128)} custom-call(s32[32]{0:T(128)} %fusion.counts_ref, s32[8192]{0:T(1024)} %bitcast.42, f32[32,8,384]{2,1,0:T(8,128)} %copy-done.5, f32[1,8,64,1152]{3,2,1,0:T(8,128)} %bitcast.41), custom_call_target="tpu_custom_call" | custom-call | tf_op jit(solution)/shard_map/deposit_rim/pallas_call | solution.py:160
  167.3 0.0 copy-start.10
  167.3 1.0 slice_bitcast_fusion.1
  168.3 0.0 slice-done
  168.3 0.1 pad_maximum_fusion
  168.4 4.6 %collective-permute-start.2 = (f32[3,8,8,1152]{3,2,1,0:T(8,128)S(1)}, f32[3,8,8,1152]{3,2,1,0:T(8,128)S(1)}, u32[]{:S(2)}, u32[]{:S(2)}) collective-permute-start(f32[3,8,8,1152]{3,2,1,0:T(8,128)S(1)} %pad_maximum_fusion), channel_id=1, source_target_pairs={{0,16},{1,17},{2,18},{3,19},{4,20},{5,21},{6,22},{7,23},{8,24},{9,... | collective-permute-start | bytes 2654216 | tf_op jit(solution)/shard_map/ppermute | solution.py:350
  173.0 1.0 slice_bitcast_fusion.2
  174.0 1.3 collective-permute-start.4
  175.3 1.0 slice.42
  176.3 1.3 collective-permute-start.3
  177.6 0.0 copy-done.10
  177.6 0.1 copy.12
  177.7 0.1 copy.13
  177.8 0.1 copy.14
  177.9 0.2 fusion.2
  178.0 0.7 reshape.64.par_ref
  178.7 0.0 collective-permute-done.3.ch_ref
  178.7 0.0 copy-start.8
  178.7 46.0 %collective-permute-done.4.cn_ref = f32[64,1152]{1,0:T(8,128)S(1)} collective-permute-done((f32[64,1152]{1,0:T(8,128)S(1)}, f32[64,1152]{1,0:T(8,128)S(1)}, u32[]{:S(2)}, u32[]{:S(2)}) %collective-permute-start.4) | collective-permute-done | bytes 294944 | tf_op jit(solution)/shard_map/ppermute | solution.py:350
  224.7 0.0 collective-permute-done.2.halo_ref
  224.7 0.0 copy-done.8
  224.7 0.7 copy-done.6
  225.4 0.9 copy-done.4
  226.3 15.6 %advance.1 = (f32[2,8,64,1152]{3,2,1,0:T(8,128)}, f32[8,8,8,1152]{3,2,1,0:T(8,128)}) custom-call(f32[32]{0:T(128)} %reshape.64.par_ref, f32[2,8,64,1152]{3,2,1,0:T(8,128)} %deposit.1.f_ref, f32[8,64,1152]{2,1,0:T(8,128)} %bitcast.40, f32[3,8,8,1152]{3,2,1,0:T(8,128)} %copy-done.4, f32[3,2,64,1152]{3,2,1,0:T(8,128)} %c_ref.1, f32[3,2,8,1152]{3,2,1,0:T(8,128)} %copy-done.8, ...), custom_call_target="tpu_custom_call" | custom-call | tf_op jit(solution)/shard_map/advance/pallas_call | solution.py:245
  241.9 11.8 %all-to-all-start.1 = ((f32[8,8,8,1152]{3,2,1,0:T(8,128)}), f32[8,8,8,1152]{3,2,1,0:T(8,128)S(1)}, u32[]{:S(2)}, u32[]{:S(2)}) async-start(f32[8,8,8,1152]{3,2,1,0:T(8,128)} %get-tuple-element.8), calls=%async_computation.1 | async-start | bytes 4718592 | tf_op jit(solution)/shard_map/all_to_all | solution.py:397
  253.7 0.1 dynamic-slice_bitcast_fusion
  253.8 0.1 copy.20
  253.8 0.6 reshape.71.lam_ref
  254.4 27.4 %all-to-all-done.1.hl_ref = f32[8,8,8,1152]{3,2,1,0:T(8,128)S(1)} async-done(((f32[8,8,8,1152]{3,2,1,0:T(8,128)}), f32[8,8,8,1152]{3,2,1,0:T(8,128)S(1)}, u32[]{:S(2)}, u32[]{:S(2)}) %all-to-all-start.1) | async-done | bytes 2359328 | tf_op jit(solution)/shard_map/all_to_all | solution.py:397
  281.8 1.4 copy-done
  283.2 2.7 cube_end.1
  285.9 1.3 collective-permute-start.5
  287.2 6.1 %collective-permute-done.5.hin_ref = f32[8,8,1152]{2,1,0:T(8,128)S(1)} collective-permute-done((f32[8,8,1152]{2,1,0:T(8,128)}, f32[8,8,1152]{2,1,0:T(8,128)S(1)}, u32[]{:S(2)}, u32[]{:S(2)}) %collective-permute-start.5) | collective-permute-done | bytes 294944 | tf_op jit(solution)/shard_map/ppermute | solution.py:350
  293.3 0.7 copy-done.7
  294.0 3.3 cube_scan.1
  297.3 10.6 %all-to-all-start.2 = ((f32[8,8,8,1152]{3,2,1,0:T(8,128)}), f32[8,8,8,1152]{3,2,1,0:T(8,128)S(1)}, u32[]{:S(2)}, u32[]{:S(2)}) async-start(f32[8,8,8,1152]{3,2,1,0:T(8,128)} %cube_scan.1), calls=%async_computation.2 | async-start | bytes 4718592 | tf_op jit(solution)/shard_map/all_to_all | solution.py:422
  308.0 0.0 copy-done.9
  308.0 0.1 copy.16
  308.0 0.1 copy.17
  308.1 0.7 reshape.66.gain_ref
  308.8 0.0 copy-done.11
  308.8 0.7 reshape.65.loss_ref
  309.5 27.4 %all-to-all-done.2.h_ref = f32[8,8,8,1152]{3,2,1,0:T(8,128)S(1)} async-done(((f32[8,8,8,1152]{3,2,1,0:T(8,128)}), f32[8,8,8,1152]{3,2,1,0:T(8,128)S(1)}, u32[]{:S(2)}, u32[]{:S(2)}) %all-to-all-start.2) | async-done | bytes 2359328 | tf_op jit(solution)/shard_map/all_to_all | solution.py:422
  336.8 1.4 copy-done.1
  338.3 20.1 %finish.1 = f32[2,8,64,1152]{3,2,1,0:T(8,128)} custom-call(f32[32]{0:T(128)} %reshape.64.par_ref, f32[64]{0:T(128)} %reshape.65.loss_ref, f32[512]{0:T(512)} %reshape.66.gain_ref, f32[2,8,64,1152]{3,2,1,0:T(8,128)} %get-tuple-element.7.adv_ref, f32[8,8,8,1152]{3,2,1,0:T(8,128)} %copy-done.1), custom_call_target="tpu_custom_call" | custom-call | tf_op jit(solution)/shard_map/finish/pallas_call | solution.py:330
  (12 shorter events, 0.1 us)
Async XLA Ops:
  1.8 157.8 %collective-permute-start.1 = (f32[8,64,1152]{2,1,0:T(8,128)S(1)}, f32[8,64,1152]{2,1,0:T(8,128)S(1)}, u32[]{:S(2)}, u32[]{:S(2)}) collective-permute-start(f32[8,64,1152]{2,1,0:T(8,128)S(1)} %slice_bitcast_fusion), channel_id=1, source_target_pairs={{0,1},{1,2},{2,3},{3,4},{4,5},{5,6},{6,7},{7,8},{8,9},{9,10},{10,1... | collective-permute-start | bytes 7077896 | tf_op jit(solution)/shard_map/ppermute | solution.py:350
  63.5 5.0 %copy-start.3 = (f32[32,8,384]{2,1,0:T(8,128)}, f32[32,8,384]{2,1,0:T(8,128)S(1)}, u32[]{:S(2)}) copy-start(f32[32,8,384]{2,1,0:T(8,128)S(1)} %all_to_all.15.slots_ref) | copy-start | bytes 1179652
  63.5 94.2 %collective-permute-start = (f32[32,8,384]{2,1,0:T(8,128)S(1)}, f32[32,8,384]{2,1,0:T(8,128)S(1)}, u32[]{:S(2)}, u32[]{:S(2)}) collective-permute-start(f32[32,8,384]{2,1,0:T(8,128)S(1)} %all_to_all.15.slots_ref), channel_id=1, source_target_pairs={{0,1},{1,2},{2,3},{3,4},{4,5},{5,6},{6,7},{7,8},{8,9},{9,10},{10,1... | collective-permute-start | bytes 1179656 | tf_op jit(solution)/shard_map/ppermute | solution.py:350
  157.7 1.9 copy-start.5
  159.6 1.4 copy-start.2
  161.0 7.3 %slice-start = ((f32[2,8,64,1152]{3,2,1,0:T(8,128)}), f32[2,8,8,1152]{3,2,1,0:T(8,128)S(1)}, s32[]{:S(2)}) async-start(f32[2,8,64,1152]{3,2,1,0:T(8,128)} %deposit.1.f_ref), calls=%async_computation.3 | async-start | bytes 1179648 | tf_op jit(solution)/shard_map/slice | solution.py:380
  167.3 10.3 %copy-start.10 = (f32[8,32]{1,0:T(8,128)S(1)}, f32[8,32]{1,0:T(8,128)}, u32[]{:S(2)}) copy-start(f32[8,32]{1,0:T(8,128)} %param.13) | copy-start | bytes 3076
  168.4 56.3 %collective-permute-start.2 = (f32[3,8,8,1152]{3,2,1,0:T(8,128)S(1)}, f32[3,8,8,1152]{3,2,1,0:T(8,128)S(1)}, u32[]{:S(2)}, u32[]{:S(2)}) collective-permute-start(f32[3,8,8,1152]{3,2,1,0:T(8,128)S(1)} %pad_maximum_fusion), channel_id=1, source_target_pairs={{0,16},{1,17},{2,18},{3,19},{4,20},{5,21},{6,22},{7,23},{8,24},{9,... | collective-permute-start | bytes 2654216 | tf_op jit(solution)/shard_map/ppermute | solution.py:350
  174.0 50.6 %collective-permute-start.4 = (f32[64,1152]{1,0:T(8,128)S(1)}, f32[64,1152]{1,0:T(8,128)S(1)}, u32[]{:S(2)}, u32[]{:S(2)}) collective-permute-start(f32[64,1152]{1,0:T(8,128)S(1)} %slice_bitcast_fusion.2), channel_id=1, source_target_pairs={{1,0},{2,1},{3,2},{4,3},{5,4},{6,5},{7,6},{8,7},{9,8},{10,9},{11,1... | collective-permute-start | bytes 884744 | tf_op jit(solution)/shard_map/ppermute | solution.py:350
  176.3 2.4 collective-permute-start.3
  178.7 46.0 %copy-start.8 = (f32[3,2,8,1152]{3,2,1,0:T(8,128)}, f32[3,2,8,1152]{3,2,1,0:T(8,128)S(1)}, u32[]{:S(2)}) copy-start(f32[3,2,8,1152]{3,2,1,0:T(8,128)S(1)} %collective-permute-done.3.ch_ref) | copy-start | bytes 663556
  224.7 0.7 copy-start.6
  225.4 0.9 copy-start.4
  241.9 39.9 %all-to-all-start.1 = ((f32[8,8,8,1152]{3,2,1,0:T(8,128)}), f32[8,8,8,1152]{3,2,1,0:T(8,128)S(1)}, u32[]{:S(2)}, u32[]{:S(2)}) async-start(f32[8,8,8,1152]{3,2,1,0:T(8,128)} %get-tuple-element.8), calls=%async_computation.1 | async-start | bytes 4718592 | tf_op jit(solution)/shard_map/all_to_all | solution.py:397
  281.8 1.4 copy-start
  285.9 7.4 %collective-permute-start.5 = (f32[8,8,1152]{2,1,0:T(8,128)}, f32[8,8,1152]{2,1,0:T(8,128)S(1)}, u32[]{:S(2)}, u32[]{:S(2)}) collective-permute-start(f32[8,8,1152]{2,1,0:T(8,128)} %cube_end.1), channel_id=1, source_target_pairs={{0,8},{1,9},{2,10},{3,11},{4,12},{5,13},{6,14},{7,15},{16,24},{17,... | collective-permute-start | bytes 884744 | tf_op jit(solution)/shard_map/ppermute | solution.py:350
  293.3 0.7 copy-start.7
  297.3 10.6 %copy-start.9 = (f32[8,8,8]{2,1,0:T(8,128)S(1)}, f32[8,8,8]{2,1,0:T(8,128)}, u32[]{:S(2)}) copy-start(f32[8,8,8]{2,1,0:T(8,128)} %param.14) | copy-start | bytes 6148
  297.3 11.5 %copy-start.11 = (f32[8,8]{1,0:T(8,128)S(1)}, f32[8,8]{1,0:T(8,128)}, u32[]{:S(2)}) copy-start(f32[8,8]{1,0:T(8,128)} %param.15) | copy-start | bytes 772
  297.3 39.5 %all-to-all-start.2 = ((f32[8,8,8,1152]{3,2,1,0:T(8,128)}), f32[8,8,8,1152]{3,2,1,0:T(8,128)S(1)}, u32[]{:S(2)}, u32[]{:S(2)}) async-start(f32[8,8,8,1152]{3,2,1,0:T(8,128)} %cube_scan.1), calls=%async_computation.2 | async-start | bytes 4718592 | tf_op jit(solution)/shard_map/all_to_all | solution.py:422
  336.8 1.4 copy-start.1
where the time goes:
time: 363 us; the launch traced here: 358 us
  Pallas kernels  141 us (39%)
  waiting for transfers between devices  107 us (29%)
  blocking collectives  52.7 us (15%)
  starting transfers between devices  39.1 us (11%)
  local copies, waits for them, and re-layouts  14.5 us (4%)
  other arithmetic  3.93 us (1%)
    pallas_call x2, Pallas kernels, deposit(): pl.pallas_call(functools.partial(deposit_kernel, row_offset), out_shape=j...  95.4 us
    all_to_all x1, blocking collectives, on_device(): lax.all_to_all(slots, ('lat', 'lev'), split_axis=0, concat_axis=0, tiled=...  52.7 us
    ppermute x6, waiting for transfers between devices, shifted(): lax.ppermute(value, axis, [(source, source + steps) for source in range(f...  52.1 us
    all_to_all x1, waiting for transfers between devices, on_device(): hl = swap(hl)  27.4 us
    all_to_all x1, waiting for transfers between devices, on_device(): h = swap(h)  27.4 us
    pallas_call x1, Pallas kernels, finish(): pl.pallas_call(finish_kernel, out_shape=jax.ShapeDtypeStruct(adv.shape, j...  20.1 us
    ppermute x6, starting transfers between devices, shifted(): lax.ppermute(value, axis, [(source, source + steps) for source in range(f...  16.7 us
    pallas_call x1, Pallas kernels, advance(): pl.pallas_call(advance_kernel, out_shape=(jax.ShapeDtypeStruct(field.shap...  15.6 us
  transfers between devices with their start and end apart: 8, of which 4 were waited for; matrix products, arithmetic and copies ran while one was open for 2% of the time, Pallas kernels for 26%

commit v1 on v0

v1 whole, which is shorter than its diff:
```python
import functools

import jax
import jax.numpy as jnp
from jax import lax
from jax.experimental import pallas as pl
from jax.experimental.pallas import tpu as pltpu
from jax.sharding import PartitionSpec as P

ADV_STEPS = 2
LANES = 128
ROUTE_BLOCK = 256
ACCS = 4
ROWS = 32
HALVES = 2
VMEM = pl.BlockSpec(memory_space=pltpu.VMEM)
SMEM = pl.BlockSpec(memory_space=pltpu.SMEM)
BIG = pltpu.CompilerParams(vmem_limit_bytes=56 * 1024 * 1024)


def cost(us):
    return pl.CostEstimate(flops=int(us * 1.1e9), bytes_accessed=int(us * 3.6e6), transcendentals=0)


def route_kernel(devices, cap_lanes, level_cells, owner_ref, cell_ref, mass_ref, out_ref, a_ref, c_ref, b_ref):
    parcels = owner_ref.shape[1]
    blocks = cap_lanes // LANES
    width = ROUTE_BLOCK
    dev_ids = lax.broadcasted_iota(jnp.int32, (devices, width), 0)
    before = (
        lax.broadcasted_iota(jnp.int32, (width, width), 0) < lax.broadcasted_iota(jnp.int32, (width, width), 1)
    ).astype(jnp.bfloat16)
    slot_ids = lax.broadcasted_iota(jnp.int32, (cap_lanes, width), 0)

    def masks(start):
        owner = owner_ref[:, pl.ds(start, width)]
        cell = cell_ref[:, pl.ds(start, width)]
        mine = owner == dev_ids
        low = cell >= level_cells
        return owner, cell, jnp.where(mine & low, 1.0, 0.0), jnp.where(mine & (~low), 1.0, 0.0)

    low_total = jnp.zeros((devices, 1), jnp.float32)
    for start in range(0, parcels, width):
        unused, unused, low, high = masks(start)
        low_total = low_total + jnp.sum(low, axis=1, keepdims=True)
    low_base = jnp.zeros((devices, 1), jnp.float32)
    high_base = low_total
    for start in range(0, parcels, width):
        owner, cell, low, high = masks(start)
        both = jnp.concatenate([low, high], axis=0)
        earlier = jnp.dot(both.astype(jnp.bfloat16), before, preferred_element_type=jnp.float32)
        rank = jnp.sum(both * (earlier + jnp.concatenate([low_base, high_base], axis=0)), axis=0, keepdims=True)
        low_base = low_base + jnp.sum(low, axis=1, keepdims=True)
        high_base = high_base + jnp.sum(high, axis=1, keepdims=True)
        b_ref[:, pl.ds(start, width)] = jnp.where(slot_ids == rank.astype(jnp.int32), 1.0, 0.0).astype(jnp.bfloat16)
        mass = mass_ref[:, pl.ds(start, width)]
        coarse = mass.astype(jnp.bfloat16).astype(jnp.float32)
        fine = mass - coarse
        owner_rows = jnp.broadcast_to(owner, (8, width))
        for device in range(0, devices, 2):
            for part, piece in enumerate((coarse, fine)):
                pair = jnp.concatenate(
                    [jnp.where(owner_rows == device + extra, piece, 0.0) for extra in range(2)], axis=0
                )
                a_ref[pl.ds(part * devices * 8 + device * 8, 16), pl.ds(start, width)] = pair.astype(jnp.bfloat16)
        mine = low + high
        for part, piece in enumerate((cell >> 16, (cell >> 8) & 255, cell & 255)):
            c_ref[pl.ds(part * devices, devices), pl.ds(start, width)] = (mine * piece.astype(jnp.float32)).astype(
                jnp.bfloat16
            )
    contract = (((1,), (1,)), ((), ()))
    sorted_mass = lax.dot_general(a_ref[...], b_ref[...], contract, preferred_element_type=jnp.float32)
    sorted_cell = lax.dot_general(c_ref[...], b_ref[...], contract, preferred_element_type=jnp.float32)
    code = (
        sorted_cell[:devices] * 65536.0 + sorted_cell[devices : 2 * devices] * 256.0 + sorted_cell[2 * devices :]
    )
    total = sorted_mass[: devices * 8] + sorted_mass[devices * 8 :]
    out_ref[:, :, pl.ds(0, cap_lanes)] = total.reshape(devices, 8, cap_lanes)
    rows = lax.broadcasted_iota(jnp.int32, (8, LANES), 0)
    for device in range(devices):
        tile = jnp.zeros((8, LANES), jnp.float32)
        for block in range(blocks):
            tile = jnp.where(rows == block, code[device : device + 1, block * LANES : (block + 1) * LANES], tile)
        tile = jnp.where(rows == blocks, high_base[device : device + 1], tile)
        tile = jnp.where(rows == blocks + 1, low_base[device : device + 1], tile)
        out_ref[device, :, pl.ds(cap_lanes, LANES)] = tile


def route(parcel_mass, parcel_owner, parcel_cell, devices, level_cells):
    parcels = parcel_owner.shape[0]
    capacity = 2 * parcels // devices
    cap_lanes = -(-capacity // LANES) * LANES
    return pl.pallas_call(
        functools.partial(route_kernel, devices, cap_lanes, level_cells),
        out_shape=jax.ShapeDtypeStruct((devices, 8, cap_lanes + LANES), jnp.float32),
        in_specs=[VMEM] * 3,
        out_specs=VMEM,
        scratch_shapes=[
            pltpu.VMEM((devices * 16, parcels), jnp.bfloat16),
            pltpu.VMEM((devices * 3, parcels), jnp.bfloat16),
            pltpu.VMEM((cap_lanes, parcels), jnp.bfloat16),
        ],
        compiler_params=BIG,
        cost_estimate=cost(4),
        name="route",
    )(parcel_owner.reshape(1, parcels), parcel_cell.reshape(1, parcels), parcel_mass)


def deposit_kernel(with_field, rows_ref, counts_ref, slots_ref, *refs):
    if with_field:
        field_ref, *refs = refs
    out_ref, list_ref, pick_ref, even_ref, odd_ref, *accs = refs
    sources, unused, width = slots_ref.shape
    cap_lanes = width - LANES
    blocks = cap_lanes // LANES
    unused, bins, lats, lons = out_ref.shape
    lon_blocks = lons // LANES
    rows = accs[0].shape[0] - 8
    step = pl.program_id(0)

    @pl.when(step == 0)
    def collect():
        def clear(index, carry):
            for acc in accs:
                acc[pl.ds(index * 8, 8)] = jnp.zeros((8, 8, LANES), jnp.float32)
            return carry

        lax.fori_loop(0, rows // 8, clear, 0)
        pick_ref[...] = jnp.where(
            lax.broadcasted_iota(jnp.int32, pick_ref.shape, 0) // 8 == lax.broadcasted_iota(jnp.int32, pick_ref.shape, 1),
            1.0,
            0.0,
        ).astype(jnp.bfloat16)
        lane_ids = lax.broadcasted_iota(jnp.int32, (LANES, LANES), 0)
        tile_row = lax.broadcasted_iota(jnp.int32, (8, LANES), 0)

        def note(source, active):
            for block in range(blocks):
                list_ref[active] = source * blocks + block
                active = active + jnp.where(counts_ref[source] > block * LANES, 1, 0)
            return active

        active = lax.fori_loop(0, sources, note, 0)
        for extra in range(3):
            list_ref[active + extra] = 0

        def spread(index, spread_ref):
            item = list_ref[index]
            source = item // blocks
            block = item % blocks
            live = jnp.where(index < active, 1.0, 0.0)
            mass = slots_ref[source, :, pl.ds(pl.multiple_of(block * LANES, LANES), LANES)] * live
            code = slots_ref[source, :, pl.ds(cap_lanes, LANES)]
            code = jnp.sum(jnp.where(tile_row == block, code, 0.0), axis=0, keepdims=True).astype(jnp.int32)
            hot = jnp.where(lane_ids == (code & (LANES - 1)), 1.0, 0.0).astype(jnp.bfloat16)
            coarse = mass.astype(jnp.bfloat16).astype(jnp.float32)
            parts = [
                pick_ref[...] * jnp.tile(jnp.concatenate([part, part], axis=0).astype(jnp.bfloat16), (LANES // 2, 1))
                for part in (coarse, mass - coarse)
            ]
            spread_ref[...] = lax.dot_general(
                jnp.concatenate(parts, axis=1),
                jnp.concatenate([hot, hot], axis=1),
                (((1,), (1,)), ((), ())),
                preferred_element_type=jnp.float32,
            )

        def add(index, spread_ref):
            base = list_ref[index] * LANES
            for first in range(0, LANES, ACCS):
                places = [rows_ref[base + first + k] for k in range(ACCS)]
                held = [acc[place] for acc, place in zip(accs, places)]
                for k in range(ACCS):
                    accs[k][places[k]] = held[k] + spread_ref[(first + k) * 8 : (first + k + 1) * 8, :]

        spread(0, even_ref)

        def pair(index, carry):
            spread(2 * index + 1, odd_ref)
            add(2 * index, even_ref)
            spread(2 * index + 2, even_ref)
            add(2 * index + 1, odd_ref)
            return carry

        lax.fori_loop(0, (active + 1) // 2, pair, 0)

    @pl.when(step > 0)
    def merge():
        flat = [acc.reshape((rows + 8) * 8, LANES) for acc in accs]
        base = (step - 1) * lats * lon_blocks * 8
        for lat in range(0, lats, 8):
            for lon in range(lon_blocks):
                at = pl.ds(lon * LANES, LANES)
                for b in range(bins):
                    picked = pl.ds(base + (lat * lon_blocks + lon) * 8 + b, 8, stride=lon_blocks * 8)
                    total = flat[0][picked, :]
                    for acc in flat[1:]:
                        total = total + acc[picked, :]
                    if with_field:
                        total = total + field_ref[0, b, pl.ds(lat, 8), at]
                    out_ref[0, b, pl.ds(lat, 8), at] = total


def deposit(field, shape, slots, cell_rows, counts, name):
    levels, bins, lats, lons = shape
    rows = levels * lats * lons // LANES
    per = lats // ROWS

    def at(step):
        block = jnp.maximum(step - 1, 0)
        return (block // per, 0, block % per, 0)

    spec = pl.BlockSpec((1, bins, ROWS, lons), at)
    fields = [] if field is None else [field]
    return pl.pallas_call(
        functools.partial(deposit_kernel, bool(fields)),
        out_shape=jax.ShapeDtypeStruct(shape, jnp.float32),
        grid=(1 + levels * per,),
        in_specs=[SMEM, SMEM, VMEM] + [spec] * len(fields),
        out_specs=spec,
        scratch_shapes=[
            pltpu.SMEM((cell_rows.shape[0] // LANES + 8,), jnp.int32),
            pltpu.VMEM((8 * LANES, LANES), jnp.bfloat16),
            pltpu.VMEM((8 * LANES, LANES), jnp.float32),
            pltpu.VMEM((8 * LANES, LANES), jnp.float32),
        ]
        + [pltpu.VMEM((rows + 8, 8, LANES), jnp.float32)] * ACCS,
        compiler_params=BIG,
        cost_estimate=cost(22 if fields else 12),
        name=name,
    )(cell_rows, counts, slots, *fields)


def advance_kernel(
    first_bin, par_ref, f_ref, rim_ref, drop_ref, halo_ref, c_ref, ch_ref, cn_ref, adv_ref, hl_ref, p0, p1, keep_ref
):
    step = pl.program_id(0)
    unused, bins, lats, lons = f_ref.shape

    @pl.when(step == 0)
    def halo():
        def one(b, carry):
            above = halo_ref[0, b]
            for level in range(2):
                f = halo_ref[1 + level, b]
                rolled = pltpu.roll(f, 1, 0)
                p0[level, b] = rolled
                new = (
                    f
                    - ch_ref[0, level] * (f - pltpu.roll(f, 1, 1))
                    - ch_ref[1, level] * (f - rolled)
                    - ch_ref[2, level] * (f - above)
                )
                p1[level, b] = pltpu.roll(new, 1, 0)
                above = f
            return carry

        lax.fori_loop(0, bins, one, 0)

    @pl.when(step > 0)
    def main():
        top_row = lax.broadcasted_iota(jnp.int32, (8, lons), 0) == 0

        def south(prev, level, b, f):
            rolled = pltpu.roll(f, 1, 0)
            out = jnp.where(top_row, prev[level, b], rolled)
            prev[level, b] = rolled
            return out

        for lat in range(lats // 8):
            at = pl.ds(lat * 8, 8)

            keep = [1.0 - c_ref[0, level, at] - c_ref[1, level, at] - c_ref[2, level, at] for level in range(2)]
            for level in range(2):
                keep_ref[level] = keep[level]

            def flow(level, b, f, prev, above):
                new = (
                    keep_ref[level] * f
                    + c_ref[0, level, at] * pltpu.roll(f, 1, 1)
                    + c_ref[1, level, at] * south(prev, level, b, f)
                )
                return new if above is None else new + c_ref[2, level, at] * above

            def one(b, carry):
                scale = first_bin + b
                f0 = f_ref[0, b, at]
                f1 = f_ref[1, b, at]
                g0 = flow(0, b, f0, p0, rim_ref[b, at] + drop_ref[b, at])
                g1 = flow(1, b, f1, p0, f0)
                a0 = flow(0, b, g0, p1, None)
                a1 = flow(1, b, g1, p1, g0)
                adv_ref[0, b, at] = a0
                adv_ref[1, b, at] = a1
                low = (a1 + par_ref[scale] * (a0 * par_ref[8 + scale])) * par_ref[24 + scale]
                hl_ref[lat, b] = cn_ref[at] * g1 + par_ref[16 + scale] * low
                return carry

            lax.fori_loop(0, bins, one, 0)


def advance(half, params, field, rim, drop, halo, courant, courant_halo, courant_next):
    levels, all_bins, lats, lons = field.shape
    bins = all_bins // HALVES
    at = lambda step: jnp.maximum(step - 1, 0)
    return pl.pallas_call(
        functools.partial(advance_kernel, half * bins),
        out_shape=(
            jax.ShapeDtypeStruct((levels, bins, lats, lons), jnp.float32),
            jax.ShapeDtypeStruct((lats // 8, bins, 8, lons), jnp.float32),
        ),
        grid=(lats // ROWS + 1,),
        in_specs=[
            SMEM,
            pl.BlockSpec((levels, bins, ROWS, lons), lambda step: (0, half, at(step), 0)),
            pl.BlockSpec((bins, ROWS, lons), lambda step: (0, at(step), 0)),
            pl.BlockSpec((bins, ROWS, lons), lambda step: (half, at(step), 0)),
            pl.BlockSpec((3, bins, 8, lons), lambda step: (0, 0, 0, 0)),
            pl.BlockSpec((3, levels, ROWS, lons), lambda step: (0, 0, at(step), 0)),
            pl.BlockSpec((3, levels, 8, lons), lambda step: (0, 0, 0, 0)),
            pl.BlockSpec((ROWS, lons), lambda step: (at(step), 0)),
        ],
        out_specs=(
            pl.BlockSpec((levels, bins, ROWS, lons), lambda step: (0, 0, at(step), 0)),
            pl.BlockSpec((ROWS // 8, bins, 8, lons), lambda step: (at(step), 0, 0, 0)),
        ),
        scratch_shapes=[pltpu.VMEM((levels, bins, 8, lons), jnp.float32)] * 2 + [pltpu.VMEM((levels, 8, lons), jnp.float32)],
        compiler_params=BIG,
        cost_estimate=cost(9),
        name="advance",
    )(params, field, rim, drop, halo, courant, courant_halo, courant_next)


def cube_end_kernel(lam_ref, hl_ref, out_ref):
    count, bins = hl_ref.shape[:2]

    def one(b, carry):
        h = hl_ref[0, b]
        for member in range(1, count):
            h = hl_ref[member, b] + lam_ref[member * bins + b] * h
        out_ref[b] = h
        return carry

    lax.fori_loop(0, bins, one, 0)


def cube_scan_kernel(lam_ref, hl_ref, hin_ref, out_ref):
    count, bins = hl_ref.shape[:2]

    def one(b, carry):
        h = hin_ref[b]
        out_ref[0, b] = h
        for member in range(count - 1):
            h = hl_ref[member, b] + lam_ref[member * bins + b] * h
            out_ref[member + 1, b] = h
        return carry

    lax.fori_loop(0, bins, one, 0)


def finish_kernel(par_ref, loss_ref, gain_ref, *refs):
    *ins, out_ref = refs
    adv_refs, h_refs = ins[:HALVES], ins[HALVES:]
    unused, bins, lats, lons = out_ref.shape
    per = bins // HALVES
    width = 3 * LANES
    parts = lons // width

    def part(index, carry):
        lat = index // parts
        row = pl.ds(pl.multiple_of(lat * 8, 8), 8)
        at = pl.ds(pl.multiple_of((index % parts) * width, LANES), width)
        above = [h_refs[b // per][lat, b % per, :, at] for b in range(bins)]
        for level in range(2):
            solved = []
            for b in range(bins):
                s = (adv_refs[b // per][level, b % per, row, at] + above[b]) * par_ref[16 * level + 8 + b]
                solved.append(s)
                above[b] = par_ref[b] * s
            for i in range(bins):
                loss = loss_ref[i * bins] * solved[0]
                for j in range(1, bins):
                    loss = loss + loss_ref[i * bins + j] * solved[j]
                total = solved[i]
                base = i * bins * bins
                for j in range(bins):
                    inner = gain_ref[base + j * bins] * solved[0]
                    for k in range(1, j + 1):
                        inner = inner + gain_ref[base + j * bins + k] * solved[k]
                    total = total + inner * solved[j]
                out_ref[level, i, row, at] = total / (1.0 + loss)
        return carry

    lax.fori_loop(0, (lats // 8) * parts, part, 0)


def finish(params, loss, gain, adv, h):
    levels, per, lats, lons = adv[0].shape
    bins = per * HALVES
    rows = ROWS // 2
    return pl.pallas_call(
        finish_kernel,
        out_shape=jax.ShapeDtypeStruct((levels, bins, lats, lons), jnp.float32),
        grid=(lats // rows,),
        in_specs=[SMEM] * 3
        + [pl.BlockSpec((levels, per, rows, lons), lambda step: (0, 0, step, 0))] * HALVES
        + [pl.BlockSpec((rows // 8, per, 8, lons), lambda step: (step, 0, 0, 0))] * HALVES,
        out_specs=pl.BlockSpec((levels, bins, rows, lons), lambda step: (0, 0, step, 0)),
        compiler_params=BIG,
        cost_estimate=cost(18),
        name="finish",
    )(params, loss, gain, *adv, *h)


def shifted(value, axis, steps):
    count = lax.axis_size(axis)
    first, last = (max(0, -steps), min(count, count - steps))
    return lax.ppermute(value, axis, [(source, source + steps) for source in range(first, last)])


def on_device(field, courant, parcel_mass, parcel_owner, parcel_cell, settle, coag_gain, coag_loss):
    levels, bins, lats, lons = field.shape
    n_lev = lax.axis_size("lev")
    devices = lax.axis_size(("lat", "lev"))
    cube = lats // 8
    cubes = n_lev // cube
    here = lax.axis_index("lev")

    per = bins // HALVES
    early_rim = shifted(field[-1, :per], "lev", 1)
    courant_next = shifted(courant[2, 0], "lev", -1)
    courant_halo = shifted(courant[:, :, -8:], "lat", 1)

    slots = route(parcel_mass, parcel_owner, parcel_cell, devices, lats * lons)
    slots = lax.all_to_all(slots, ("lat", "lev"), split_axis=0, concat_axis=0, tiled=True)
    cap_lanes = slots.shape[2] - LANES
    blocks = cap_lanes // LANES
    level_rows = lats * lons // LANES
    rim_slots = shifted(slots, "lev", 1)

    def tables(slots, row):
        codes = slots[:, :blocks, cap_lanes:].astype(jnp.int32).reshape(devices * cap_lanes)
        counts = slots[:, row, cap_lanes].astype(jnp.int32)
        return codes // LANES, counts

    rows, counts = tables(slots, blocks)
    f0 = deposit(field, field.shape, slots, rows, counts, "deposit")
    rim_slots, later_rim = lax.optimization_barrier((rim_slots, field[-1, per:]))
    raw_rims = [early_rim, shifted(later_rim, "lev", 1)]
    rows, counts = tables(rim_slots, blocks + 1)
    rows = jnp.where(rows < level_rows, level_rows, rows - level_rows)
    drop = deposit(None, (1,) + field.shape[1:], rim_slots, rows, counts, "deposit_rim")[0]
    pairs = settle.reshape(bins, n_lev, 2)
    first, second = pairs[:, :, 0], pairs[:, :, 1]
    table = jnp.stack([first, 1.0 / (1.0 + first), second, 1.0 / (1.0 + second)], axis=0)
    params = lax.dynamic_index_in_dim(table, here, axis=2, keepdims=False).reshape(4 * bins)
    lam = (table[0] * table[1] * table[2] * table[3]).T
    lam = lax.dynamic_slice_in_dim(lam, here // cube * cube, cube, axis=0)
    gain = coag_gain + jnp.swapaxes(coag_gain, 1, 2)
    gain = jnp.where(jnp.eye(bins, dtype=bool)[None], coag_gain, gain)

    groups = [list(range(c * cube, (c + 1) * cube)) for c in range(cubes)]
    swap = functools.partial(
        lax.all_to_all, axis_name="lev", split_axis=0, concat_axis=0, axis_index_groups=groups, tiled=True
    )
    advs, hs = [], []
    for half in range(HALVES):
        own = slice(half * per, (half + 1) * per)
        raw_rim = raw_rims[half]
        if half:
            advs[-1], raw_rim = lax.optimization_barrier((advs[-1], raw_rim))
        rim_halo = raw_rim[:, -8:] + drop[own, -8:]
        halo = shifted(jnp.concatenate([rim_halo[None], f0[:, own, -8:]], axis=0), "lat", 1)
        adv, hl = advance(half, params, f0, raw_rim, drop, halo, courant, courant_halo, courant_next)
        advs.append(adv)
        hs.append(swap(hl))
    for half in range(HALVES):
        hs[half] = swap(carry_scan(hs[half], lam[:, half * per : (half + 1) * per], cubes))
    return finish(params, coag_loss.reshape(-1), gain.reshape(-1), advs, hs)


def carry_scan(hl, lam, cubes):
    cube = hl.shape[0]
    flat_lam = lam.reshape(-1)
    end = pl.pallas_call(
        cube_end_kernel,
        out_shape=jax.ShapeDtypeStruct(hl.shape[1:], jnp.float32),
        in_specs=[SMEM, VMEM],
        out_specs=VMEM,
        compiler_params=BIG,
        cost_estimate=cost(2),
        name="cube_end",
    )(flat_lam, hl)
    reach = 1
    factor = jnp.prod(lam, axis=0)[:, None, None]
    while reach < cubes - 1:
        end = end + factor * shifted(end, "lev", reach * cube)
        factor = factor * shifted(factor, "lev", reach * cube)
        reach = 2 * reach
    carried = shifted(end, "lev", cube)
    return pl.pallas_call(
        cube_scan_kernel,
        out_shape=jax.ShapeDtypeStruct(hl.shape, jnp.float32),
        in_specs=[SMEM, VMEM, VMEM],
        out_specs=VMEM,
        compiler_params=BIG,
        cost_estimate=cost(2),
        name="cube_scan",
    )(flat_lam, hl, carried)


def solution(mesh):
    in_specs = (
        P("lev", None, "lat", None),
        P(None, "lev", "lat", None),
        P(None, ("lat", "lev")),
        P(("lat", "lev"), None),
        P(("lat", "lev")),
        P(),
        P(),
        P(),
    )
    out_specs = P("lev", None, "lat", None)
    return jax.shard_map(
        on_device, mesh=mesh, in_specs=in_specs, out_specs=out_specs, check_vma=False
    )
```

time: 363 us -> 209 us (0.58)
  waiting for transfers between devices: 107 us -> 45.5 us
  Pallas kernels: 141 us -> 79.9 us
  blocking collectives: 52.7 us -> 0 us
  starting transfers between devices: 39.1 us -> 61.8 us
    pallas_call x6 -> x9, Pallas kernels: 137 us -> 75.9 us  [the longest x2 26.6 us: deposit(): pl.pallas_call(functools.partial(deposit_kernel, bool(fields)), out_shape...]
    all_to_all x1 -> x0, blocking collectives: 52.7 us -> none  [on_device(): lax.all_to_all(slots, ('lat', 'lev'), split_axis=0, concat_axis=0, tiled=...]
    all_to_all x2 -> x5, waiting for transfers between devices: 54.7 us -> 18.1 us  [the longest x2 12.4 us: on_device(): swap(carry_scan(hs[half], lam[:, half * per:(half + 1) * per], cubes))]
    ppermute x6 -> x9, waiting for transfers between devices: 52.1 us -> 27.4 us  [shifted(): lax.ppermute(value, axis, [(source, source + steps) for source in range(f...]
    ppermute x6 -> x9, starting transfers between devices: 16.7 us -> 28.9 us  [shifted(): lax.ppermute(value, axis, [(source, source + steps) for source in range(f...]
    all_to_all x2 -> x5, starting transfers between devices: 22.4 us -> 32.9 us  [the longest x2 18.2 us: on_device(): hs.append(swap(hl))]
  transfers between devices with their start and end apart: 8 -> 14, of which waited for: 4 -> 8; matrix products, arithmetic and copies ran while one was open for 2% -> 7% of each run, Pallas kernels for 26% -> 28%
where the time goes in v1:
time: 209 us; the launch traced here: 208 us
  Pallas kernels  79.9 us (38%)
  starting transfers between devices  61.8 us (30%)
  waiting for transfers between devices  45.5 us (22%)
  local copies, waits for them, and re-layouts  14.4 us (7%)
  other arithmetic  5.99 us (3%)
    ppermute x9, starting transfers between devices, shifted(): lax.ppermute(value, axis, [(source, source + steps) for source in range(f...  28.9 us
    ppermute x9, waiting for transfers between devices, shifted(): lax.ppermute(value, axis, [(source, source + steps) for source in range(f...  27.4 us
    pallas_call x2, Pallas kernels, deposit(): pl.pallas_call(functools.partial(deposit_kernel, bool(fields)), out_shape...  26.6 us
    pallas_call x1, Pallas kernels, finish(): pl.pallas_call(finish_kernel, out_shape=jax.ShapeDtypeStruct((levels, bin...  20.7 us
    pallas_call x2, Pallas kernels, advance(): pl.pallas_call(functools.partial(advance_kernel, half * bins), out_shape=...  19.7 us
    all_to_all x2, starting transfers between devices, on_device(): hs.append(swap(hl))  18.2 us
    all_to_all x2, waiting for transfers between devices, on_device(): swap(carry_scan(hs[half], lam[:, half * per:(half + 1) * per], cubes))  12.4 us
    all_to_all x2, starting transfers between devices, on_device(): swap(carry_scan(hs[half], lam[:, half * per:(half + 1) * per], cubes))  8.01 us
  transfers between devices with their start and end apart: 14, of which 8 were waited for; matrix products, arithmetic and copies ran while one was open for 7% of the time, Pallas kernels for 28%

profile of v1, /device:TPU:0, one launch (start us, length us, event | category | flops | bytes accessed | tf_op | source)
XLA Modules:
  0.0 207.8 jit_solution(4895682283919021258)
XLA Ops:
  0.0 1.6 slice.65
  1.6 3.0 %collective-permute-start.3 = (f32[3,2,8,1152]{3,2,1,0:T(8,128)}, f32[3,2,8,1152]{3,2,1,0:T(8,128)}, u32[]{:S(2)}, u32[]{:S(2)}) collective-permute-start(f32[3,2,8,1152]{3,2,1,0:T(8,128)} %slice.65), channel_id=1, source_target_pairs={{0,16},{1,17},{2,18},{3,19},{4,20},{5,21},{6,22},{7,23},{8,24},{9,... | collective-permute-start | bytes 663560 | tf_op jit(solution)/shard_map/ppermute | solution.py:418
  4.7 4.0 %route.1 = f32[32,8,384]{2,1,0:T(8,128)} custom-call(s32[1,4096]{1,0:T(1,128)} %bitcast.51, s32[1,4096]{1,0:T(1,128)} %bitcast.52, f32[8,4096]{1,0:T(8,128)} %mass_ref.1), custom_call_target="tpu_custom_call" | custom-call | flops 4400000000 | bytes 14400000 | tf_op jit(solution)/shard_map/route/pallas_call | solution.py:93
  8.7 6.7 %all-to-all-start = ((f32[32,8,384]{2,1,0:T(8,128)}), f32[32,8,384]{2,1,0:T(8,128)S(1)}, u32[]{:S(2)}, u32[]{:S(2)}) async-start(f32[32,8,384]{2,1,0:T(8,128)} %route.1), calls=%async_computation | async-start | bytes 786432 | tf_op jit(solution)/shard_map/all_to_all | solution.py:435
  15.4 1.0 slice_bitcast_fusion.2
  16.3 0.0 copy-start.7
  16.4 1.3 collective-permute-start.4
  17.7 1.8 slice_bitcast_fusion
  19.5 5.6 %collective-permute-start = (f32[4,64,1152]{2,1,0:T(8,128)S(1)}, f32[4,64,1152]{2,1,0:T(8,128)}, u32[]{:S(2)}, u32[]{:S(2)}) collective-permute-start(f32[4,64,1152]{2,1,0:T(8,128)S(1)} %get-tuple-element.24), channel_id=1, source_target_pairs={{0,1},{1,2},{2,3},{3,4},{4,5},{5,6},{6,7},{7,8},{8,9},{9,10},{10,1... | collective-permute-start | bytes 3538952 | tf_op jit(solution)/shard_map/ppermute | solution.py:418
  25.0 0.1 copy.13
  25.1 4.3 %all-to-all-done.slots_ref = f32[32,8,384]{2,1,0:T(8,128)S(1)} async-done(((f32[32,8,384]{2,1,0:T(8,128)}), f32[32,8,384]{2,1,0:T(8,128)S(1)}, u32[]{:S(2)}, u32[]{:S(2)}) %all-to-all-start) | async-done | bytes 393248 | tf_op jit(solution)/shard_map/all_to_all | solution.py:435
  29.4 0.7 add_select_fusion.1.rows_ref
  30.1 1.2 fusion.6.counts_ref
  31.3 2.2 %collective-permute-start.1 = (f32[32,8,384]{2,1,0:T(8,128)S(1)}, f32[32,8,384]{2,1,0:T(8,128)S(1)}, u32[]{:S(2)}, u32[]{:S(2)}) collective-permute-start(f32[32,8,384]{2,1,0:T(8,128)S(1)} %all-to-all-done.slots_ref), channel_id=1, source_target_pairs={{0,1},{1,2},{2,3},{3,4},{4,5},{5,6},{6,7},{7,8},{8,9},{9,10},{10,1... | collective-permute-start | bytes 1179656 | tf_op jit(solution)/shard_map/ppermute | solution.py:418
  33.5 21.4 %deposit.1.f_ref = f32[2,8,64,1152]{3,2,1,0:T(8,128)} custom-call(s32[8192]{0:T(1024)} %add_select_fusion.1.rows_ref, s32[32]{0:T(128)} %fusion.6.counts_ref, f32[32,8,384]{2,1,0:T(8,128)} %copy-done.4, f32[2,8,64,1152]{3,2,1,0:T(8,128)} %refs_0_.1), custom_call_target="tpu_custom_call" | custom-call | flops 24199999488 | bytes 79200000 | tf_op jit(solution)/shard_map/deposit/pallas_call | solution.py:215
  54.9 1.1 fusion.11
  56.0 7.6 %collective-permute-done.1.slots_ref = f32[32,8,384]{2,1,0:T(8,128)S(1)} collective-permute-done((f32[32,8,384]{2,1,0:T(8,128)S(1)}, f32[32,8,384]{2,1,0:T(8,128)S(1)}, u32[]{:S(2)}, u32[]{:S(2)}) %collective-permute-start.1) | collective-permute-done | bytes 393248 | tf_op jit(solution)/shard_map/ppermute | solution.py:418
  63.7 1.2 convert_reduce_fusion.counts_ref
  64.8 0.6 add_select_fusion.3.rows_ref
  65.5 5.5 %collective-permute-start.5 = (f32[4,64,1152]{2,1,0:T(8,128)S(1)}, f32[4,64,1152]{2,1,0:T(8,128)}, u32[]{:S(2)}, u32[]{:S(2)}) collective-permute-start(f32[4,64,1152]{2,1,0:T(8,128)S(1)} %get-tuple-element.15), channel_id=1, source_target_pairs={{0,1},{1,2},{2,3},{3,4},{4,5},{5,6},{6,7},{7,8},{8,9},{9,10},{10,1... | collective-permute-start | bytes 3538952 | tf_op jit(solution)/shard_map/ppermute | solution.py:418
  71.0 5.1 %deposit_rim.1 = f32[1,8,64,1152]{3,2,1,0:T(8,128)} custom-call(s32[8192]{0:T(1024)} %add_select_fusion.3.rows_ref, s32[32]{0:T(128)} %convert_reduce_fusion.counts_ref, f32[32,8,384]{2,1,0:T(8,128)} %copy-done.6), custom_call_target="tpu_custom_call" | custom-call | flops 13200000000 | bytes 43200000 | tf_op jit(solution)/shard_map/deposit_rim/pallas_call | solution.py:215
  76.1 0.0 collective-permute-done.rim_ref
  76.1 1.0 fusion.1
  77.1 1.7 collective-permute-start.2
  78.8 0.1 copy.14
  78.9 0.1 copy.15
  79.0 0.2 fusion.7
  79.1 0.7 reshape.67.par_ref
  79.8 0.3 collective-permute-done.2.halo_ref
  80.2 0.8 copy-done.9
  80.9 9.8 %advance.2 = (f32[2,4,64,1152]{3,2,1,0:T(8,128)}, f32[8,4,8,1152]{3,2,1,0:T(8,128)}) custom-call(f32[32]{0:T(128)} %reshape.67.par_ref, f32[2,8,64,1152]{3,2,1,0:T(8,128)} %deposit.1.f_ref, f32[4,64,1152]{2,1,0:T(8,128)} %collective-permute-done.rim_ref, f32[8,64,1152]{2,1,0:T(8,128)} %bitcast.48, f32[3,4,8,1152]{3,2,1,0:T(8,128)} %copy-done.9, ...), custom_call_target="tpu_custom_call" | custom-call | flops 9900000256 | bytes 32400000 | tf_op jit(solution)/shard_map/advance/pallas_call | solution.py:306
  90.8 14.4 %all-to-all-start.1 = ((f32[8,4,8,1152]{3,2,1,0:T(8,128)}), f32[8,4,8,1152]{3,2,1,0:T(8,128)S(1)}, u32[]{:S(2)}, u32[]{:S(2)}) async-start(f32[8,4,8,1152]{3,2,1,0:T(8,128)} %get-tuple-element.19), calls=%async_computation.1 | async-start | bytes 2359296 | tf_op jit(solution)/shard_map/all_to_all | solution.py:476
  105.2 1.0 fusion
  106.2 2.0 collective-permute-start.6
  108.3 1.4 collective-permute-done.6.halo_ref
  109.6 0.8 copy-done.10
  110.4 9.8 %advance.3 = (f32[2,4,64,1152]{3,2,1,0:T(8,128)}, f32[8,4,8,1152]{3,2,1,0:T(8,128)}) custom-call(f32[32]{0:T(128)} %reshape.67.par_ref, f32[2,8,64,1152]{3,2,1,0:T(8,128)} %deposit.1.f_ref, f32[4,64,1152]{2,1,0:T(8,128)} %collective-permute-done.5.rim_ref, f32[8,64,1152]{2,1,0:T(8,128)} %bitcast.50, f32[3,4,8,1152]{3,2,1,0:T(8,128)} %copy-done.10, ...), custom_call_target="tpu_custom_call" | custom-call | flops 9900000256 | bytes 32400000 | tf_op jit(solution)/shard_map/advance/pallas_call | solution.py:306
  120.2 1.5 all-to-all-done.1.hl_ref
  121.7 1.0 copy-done
  122.7 3.8 %all-to-all-start.3 = ((f32[8,4,8,1152]{3,2,1,0:T(8,128)}), f32[8,4,8,1152]{3,2,1,0:T(8,128)S(1)}, u32[]{:S(2)}, u32[]{:S(2)}) async-start(f32[8,4,8,1152]{3,2,1,0:T(8,128)} %get-tuple-element.20), calls=%async_computation.3 | async-start | bytes 2359296 | tf_op jit(solution)/shard_map/all_to_all | solution.py:476
  126.5 0.1 dynamic-slice_bitcast_fusion
  126.6 0.1 copy.21
  126.7 0.6 reshape.74.lam_ref
  127.3 2.1 cube_end.2
  129.4 2.5 %collective-permute-start.7 = (f32[4,8,1152]{2,1,0:T(8,128)}, f32[4,8,1152]{2,1,0:T(8,128)S(1)}, u32[]{:S(2)}, u32[]{:S(2)}) collective-permute-start(f32[4,8,1152]{2,1,0:T(8,128)} %cube_end.2), channel_id=1, source_target_pairs={{0,8},{1,9},{2,10},{3,11},{4,12},{5,13},{6,14},{7,15},{16,24},{17,... | collective-permute-start | bytes 442376 | tf_op jit(solution)/shard_map/ppermute | solution.py:418
  131.9 10.8 %collective-permute-done.7.hin_ref = f32[4,8,1152]{2,1,0:T(8,128)S(1)} collective-permute-done((f32[4,8,1152]{2,1,0:T(8,128)}, f32[4,8,1152]{2,1,0:T(8,128)S(1)}, u32[]{:S(2)}, u32[]{:S(2)}) %collective-permute-start.7) | collective-permute-done | bytes 147488 | tf_op jit(solution)/shard_map/ppermute | solution.py:418
  142.8 0.7 copy-done.11
  143.4 2.4 %cube_scan.2 = f32[8,4,8,1152]{3,2,1,0:T(8,128)} custom-call(f32[32]{0:T(128)} %reshape.74.lam_ref, f32[8,4,8,1152]{3,2,1,0:T(8,128)} %copy-done, f32[4,8,1152]{2,1,0:T(8,128)} %copy-done.11), custom_call_target="tpu_custom_call" | custom-call | flops 2200000000 | bytes 7200000 | tf_op jit(solution)/shard_map/cube_scan/pallas_call | solution.py:501
  145.9 4.1 %all-to-all-start.2 = ((f32[8,4,8,1152]{3,2,1,0:T(8,128)}), f32[8,4,8,1152]{3,2,1,0:T(8,128)S(1)}, u32[]{:S(2)}, u32[]{:S(2)}) async-start(f32[8,4,8,1152]{3,2,1,0:T(8,128)} %cube_scan.2), calls=%async_computation.2 | async-start | bytes 2359296 | tf_op jit(solution)/shard_map/all_to_all | solution.py:478
  150.0 0.1 copy.22
  150.1 0.7 reshape.75.lam_ref
  150.7 2.1 cube_end.3
  152.8 5.2 %collective-permute-start.8 = (f32[4,8,1152]{2,1,0:T(8,128)}, f32[4,8,1152]{2,1,0:T(8,128)S(1)}, u32[]{:S(2)}, u32[]{:S(2)}) collective-permute-start(f32[4,8,1152]{2,1,0:T(8,128)} %cube_end.3), channel_id=1, source_target_pairs={{0,8},{1,9},{2,10},{3,11},{4,12},{5,13},{6,14},{7,15},{16,24},{17,... | collective-permute-start | bytes 442376 | tf_op jit(solution)/shard_map/ppermute | solution.py:418
  158.0 7.2 %collective-permute-done.8.hin_ref = f32[4,8,1152]{2,1,0:T(8,128)S(1)} collective-permute-done((f32[4,8,1152]{2,1,0:T(8,128)}, f32[4,8,1152]{2,1,0:T(8,128)S(1)}, u32[]{:S(2)}, u32[]{:S(2)}) %collective-permute-start.8) | collective-permute-done | bytes 147488 | tf_op jit(solution)/shard_map/ppermute | solution.py:418
  165.2 0.7 copy-done.12
  165.8 2.4 %cube_scan.3 = f32[8,4,8,1152]{3,2,1,0:T(8,128)} custom-call(f32[32]{0:T(128)} %reshape.75.lam_ref, f32[8,4,8,1152]{3,2,1,0:T(8,128)} %copy-done.1, f32[4,8,1152]{2,1,0:T(8,128)} %copy-done.12), custom_call_target="tpu_custom_call" | custom-call | flops 2200000000 | bytes 7200000 | tf_op jit(solution)/shard_map/cube_scan/pallas_call | solution.py:501
  168.3 3.9 %all-to-all-start.4 = ((f32[8,4,8,1152]{3,2,1,0:T(8,128)}), f32[8,4,8,1152]{3,2,1,0:T(8,128)S(1)}, u32[]{:S(2)}, u32[]{:S(2)}) async-start(f32[8,4,8,1152]{3,2,1,0:T(8,128)} %cube_scan.3), calls=%async_computation.4 | async-start | bytes 2359296 | tf_op jit(solution)/shard_map/all_to_all | solution.py:478
  172.2 0.7 reshape.68.loss_ref
  172.8 0.1 copy.17
  172.9 0.1 copy.18
  173.0 0.7 reshape.69.gain_ref
  173.7 12.4 %all-to-all-done.4.refs_3_ = f32[8,4,8,1152]{3,2,1,0:T(8,128)S(1)} async-done(((f32[8,4,8,1152]{3,2,1,0:T(8,128)}), f32[8,4,8,1152]{3,2,1,0:T(8,128)S(1)}, u32[]{:S(2)}, u32[]{:S(2)}) %all-to-all-start.4) | async-done | bytes 1179680 | tf_op jit(solution)/shard_map/all_to_all | solution.py:478
  186.1 1.1 copy-done.3
  187.1 20.7 %finish.1 = f32[2,8,64,1152]{3,2,1,0:T(8,128)} custom-call(f32[32]{0:T(128)} %reshape.67.par_ref, f32[64]{0:T(128)} %reshape.68.loss_ref, f32[512]{0:T(512)} %reshape.69.gain_ref, f32[2,4,64,1152]{3,2,1,0:T(8,128)} %get-tuple-element.16.refs_0_, f32[2,4,64,1152]{3,2,1,0:T(8,128)} %get-tuple-element.18.refs_1_, f32[8,4,8,1152]{3,2,1,0:T(8,128)} %copy-done.2, ...), custom_call_target="tpu_custom_call" | custom-call | flops 19800000512 | bytes 64800000 | tf_op jit(solution)/shard_map/finish/pallas_call | solution.py:401
  (34 shorter events, 0.2 us)
Async XLA Ops:
  1.6 78.2 %collective-permute-start.3 = (f32[3,2,8,1152]{3,2,1,0:T(8,128)}, f32[3,2,8,1152]{3,2,1,0:T(8,128)}, u32[]{:S(2)}, u32[]{:S(2)}) collective-permute-start(f32[3,2,8,1152]{3,2,1,0:T(8,128)} %slice.65), channel_id=1, source_target_pairs={{0,16},{1,17},{2,18},{3,19},{4,20},{5,21},{6,22},{7,23},{8,24},{9,... | collective-permute-start | bytes 663560 | tf_op jit(solution)/shard_map/ppermute | solution.py:418
  8.7 20.7 %all-to-all-start = ((f32[32,8,384]{2,1,0:T(8,128)}), f32[32,8,384]{2,1,0:T(8,128)S(1)}, u32[]{:S(2)}, u32[]{:S(2)}) async-start(f32[32,8,384]{2,1,0:T(8,128)} %route.1), calls=%async_computation | async-start | bytes 786432 | tf_op jit(solution)/shard_map/all_to_all | solution.py:435
  16.3 8.7 %copy-start.7 = (f32[8,32]{1,0:T(8,128)S(1)}, f32[8,32]{1,0:T(8,128)}, u32[]{:S(2)}) copy-start(f32[8,32]{1,0:T(8,128)} %param.13) | copy-start | bytes 3076
  16.4 63.5 %collective-permute-start.4 = (f32[64,1152]{1,0:T(8,128)S(1)}, f32[64,1152]{1,0:T(8,128)}, u32[]{:S(2)}, u32[]{:S(2)}) collective-permute-start(f32[64,1152]{1,0:T(8,128)S(1)} %slice_bitcast_fusion.2), channel_id=1, source_target_pairs={{1,0},{2,1},{3,2},{4,3},{5,4},{6,5},{7,6},{8,7},{9,8},{10,9},{11,1... | collective-permute-start | bytes 884744 | tf_op jit(solution)/shard_map/ppermute | solution.py:418
  19.5 56.6 %collective-permute-start = (f32[4,64,1152]{2,1,0:T(8,128)S(1)}, f32[4,64,1152]{2,1,0:T(8,128)}, u32[]{:S(2)}, u32[]{:S(2)}) collective-permute-start(f32[4,64,1152]{2,1,0:T(8,128)S(1)} %get-tuple-element.24), channel_id=1, source_target_pairs={{0,1},{1,2},{2,3},{3,4},{4,5},{5,6},{6,7},{7,8},{8,9},{9,10},{10,1... | collective-permute-start | bytes 3538952 | tf_op jit(solution)/shard_map/ppermute | solution.py:418
  29.4 4.1 %copy-start.4 = (f32[32,8,384]{2,1,0:T(8,128)}, f32[32,8,384]{2,1,0:T(8,128)S(1)}, u32[]{:S(2)}) copy-start(f32[32,8,384]{2,1,0:T(8,128)S(1)} %all-to-all-done.slots_ref) | copy-start | bytes 1179652
  31.3 32.3 %collective-permute-start.1 = (f32[32,8,384]{2,1,0:T(8,128)S(1)}, f32[32,8,384]{2,1,0:T(8,128)S(1)}, u32[]{:S(2)}, u32[]{:S(2)}) collective-permute-start(f32[32,8,384]{2,1,0:T(8,128)S(1)} %all-to-all-done.slots_ref), channel_id=1, source_target_pairs={{0,1},{1,2},{2,3},{3,4},{4,5},{5,6},{6,7},{7,8},{8,9},{9,10},{10,1... | collective-permute-start | bytes 1179656 | tf_op jit(solution)/shard_map/ppermute | solution.py:418
  63.7 7.3 %copy-start.6 = (f32[32,8,384]{2,1,0:T(8,128)}, f32[32,8,384]{2,1,0:T(8,128)S(1)}, u32[]{:S(2)}) copy-start(f32[32,8,384]{2,1,0:T(8,128)S(1)} %collective-permute-done.1.slots_ref) | copy-start | bytes 1179652
  65.5 39.7 %collective-permute-start.5 = (f32[4,64,1152]{2,1,0:T(8,128)S(1)}, f32[4,64,1152]{2,1,0:T(8,128)}, u32[]{:S(2)}, u32[]{:S(2)}) collective-permute-start(f32[4,64,1152]{2,1,0:T(8,128)S(1)} %get-tuple-element.15), channel_id=1, source_target_pairs={{0,1},{1,2},{2,3},{3,4},{4,5},{5,6},{6,7},{7,8},{8,9},{9,10},{10,1... | collective-permute-start | bytes 3538952 | tf_op jit(solution)/shard_map/ppermute | solution.py:418
  77.1 3.1 %collective-permute-start.2 = (f32[3,4,8,1152]{3,2,1,0:T(8,128)S(1)}, f32[3,4,8,1152]{3,2,1,0:T(8,128)S(1)}, u32[]{:S(2)}, u32[]{:S(2)}) collective-permute-start(f32[3,4,8,1152]{3,2,1,0:T(8,128)S(1)} %pad_maximum_fusion), channel_id=1, source_target_pairs={{0,16},{1,17},{2,18},{3,19},{4,20},{5,21},{6,22},{7,23},{8,24},{9,... | collective-permute-start | bytes 1327112 | tf_op jit(solution)/shard_map/ppermute | solution.py:418
  80.2 0.8 copy-start.9
  90.8 30.9 %all-to-all-start.1 = ((f32[8,4,8,1152]{3,2,1,0:T(8,128)}), f32[8,4,8,1152]{3,2,1,0:T(8,128)S(1)}, u32[]{:S(2)}, u32[]{:S(2)}) async-start(f32[8,4,8,1152]{3,2,1,0:T(8,128)} %get-tuple-element.19), calls=%async_computation.1 | async-start | bytes 2359296 | tf_op jit(solution)/shard_map/all_to_all | solution.py:476
  106.2 3.4 %collective-permute-start.6 = (f32[3,4,8,1152]{3,2,1,0:T(8,128)S(1)}, f32[3,4,8,1152]{3,2,1,0:T(8,128)S(1)}, u32[]{:S(2)}, u32[]{:S(2)}) collective-permute-start(f32[3,4,8,1152]{3,2,1,0:T(8,128)S(1)} %pad_maximum_fusion.1), channel_id=1, source_target_pairs={{0,16},{1,17},{2,18},{3,19},{4,20},{5,21},{6,22},{7,23},{8,24},{9,... | collective-permute-start | bytes 1327112 | tf_op jit(solution)/shard_map/ppermute | solution.py:418
  109.6 0.8 copy-start.10
  121.7 1.0 copy-start
  122.7 23.1 %all-to-all-start.3 = ((f32[8,4,8,1152]{3,2,1,0:T(8,128)}), f32[8,4,8,1152]{3,2,1,0:T(8,128)S(1)}, u32[]{:S(2)}, u32[]{:S(2)}) async-start(f32[8,4,8,1152]{3,2,1,0:T(8,128)} %get-tuple-element.20), calls=%async_computation.3 | async-start | bytes 2359296 | tf_op jit(solution)/shard_map/all_to_all | solution.py:476
  129.4 13.4 %collective-permute-start.7 = (f32[4,8,1152]{2,1,0:T(8,128)}, f32[4,8,1152]{2,1,0:T(8,128)S(1)}, u32[]{:S(2)}, u32[]{:S(2)}) collective-permute-start(f32[4,8,1152]{2,1,0:T(8,128)} %cube_end.2), channel_id=1, source_target_pairs={{0,8},{1,9},{2,10},{3,11},{4,12},{5,13},{6,14},{7,15},{16,24},{17,... | collective-permute-start | bytes 442376 | tf_op jit(solution)/shard_map/ppermute | solution.py:418
  142.8 0.7 copy-start.11
  145.9 4.1 %copy-start.1 = (f32[8,4,8,1152]{3,2,1,0:T(8,128)}, f32[8,4,8,1152]{3,2,1,0:T(8,128)S(1)}, u32[]{:S(2)}) copy-start(f32[8,4,8,1152]{3,2,1,0:T(8,128)S(1)} %all-to-all-done.3.hl_ref) | copy-start | bytes 3538948
  145.9 22.4 %all-to-all-start.2 = ((f32[8,4,8,1152]{3,2,1,0:T(8,128)}), f32[8,4,8,1152]{3,2,1,0:T(8,128)S(1)}, u32[]{:S(2)}, u32[]{:S(2)}) async-start(f32[8,4,8,1152]{3,2,1,0:T(8,128)} %cube_scan.2), calls=%async_computation.2 | async-start | bytes 2359296 | tf_op jit(solution)/shard_map/all_to_all | solution.py:478
  152.8 12.3 %collective-permute-start.8 = (f32[4,8,1152]{2,1,0:T(8,128)}, f32[4,8,1152]{2,1,0:T(8,128)S(1)}, u32[]{:S(2)}, u32[]{:S(2)}) collective-permute-start(f32[4,8,1152]{2,1,0:T(8,128)} %cube_end.3), channel_id=1, source_target_pairs={{0,8},{1,9},{2,10},{3,11},{4,12},{5,13},{6,14},{7,15},{16,24},{17,... | collective-permute-start | bytes 442376 | tf_op jit(solution)/shard_map/ppermute | solution.py:418
  165.2 0.7 copy-start.12
  168.3 3.9 %copy-start.8 = (f32[8,8]{1,0:T(8,128)S(1)}, f32[8,8]{1,0:T(8,128)}, u32[]{:S(2)}) copy-start(f32[8,8]{1,0:T(8,128)} %param.15) | copy-start | bytes 772
  168.3 4.6 %copy-start.5 = (f32[8,8,8]{2,1,0:T(8,128)S(1)}, f32[8,8,8]{2,1,0:T(8,128)}, u32[]{:S(2)}) copy-start(f32[8,8,8]{2,1,0:T(8,128)} %param.14) | copy-start | bytes 6148
  168.3 4.6 %copy-start.2 = (f32[8,4,8,1152]{3,2,1,0:T(8,128)}, f32[8,4,8,1152]{3,2,1,0:T(8,128)S(1)}, u32[]{:S(2)}) copy-start(f32[8,4,8,1152]{3,2,1,0:T(8,128)S(1)} %all-to-all-done.2.refs_2_) | copy-start | bytes 3538948
  168.3 17.8 %all-to-all-start.4 = ((f32[8,4,8,1152]{3,2,1,0:T(8,128)}), f32[8,4,8,1152]{3,2,1,0:T(8,128)S(1)}, u32[]{:S(2)}, u32[]{:S(2)}) async-start(f32[8,4,8,1152]{3,2,1,0:T(8,128)} %cube_scan.3), calls=%async_computation.4 | async-start | bytes 2359296 | tf_op jit(solution)/shard_map/all_to_all | solution.py:478
  186.1 1.1 copy-start.3

commit v2 on v1

--- a/solution.py
+++ b/solution.py
@@ -358,43 +358,53 @@
     lax.fori_loop(0, bins, one, 0)
 
 
-def finish_kernel(par_ref, loss_ref, gain_ref, *refs):
+def finish_kernel(par_ref, mix_ref, *refs):
     *ins, out_ref = refs
     adv_refs, h_refs = ins[:HALVES], ins[HALVES:]
     unused, bins, lats, lons = out_ref.shape
     per = bins // HALVES
-    width = 3 * LANES
-    parts = lons // width
+    tiles = range(lats // 8)
 
     def part(index, carry):
-        lat = index // parts
-        row = pl.ds(pl.multiple_of(lat * 8, 8), 8)
-        at = pl.ds(pl.multiple_of((index % parts) * width, LANES), width)
-        above = [h_refs[b // per][lat, b % per, :, at] for b in range(bins)]
+        at = pl.ds(pl.multiple_of(index * LANES, LANES), LANES)
+        above = [jnp.concatenate([h_refs[b // per][t, b % per, :, at] for t in tiles], axis=1) for b in range(bins)]
         for level in range(2):
             solved = []
             for b in range(bins):
-                s = (adv_refs[b // per][level, b % per, row, at] + above[b]) * par_ref[16 * level + 8 + b]
+                adv = [adv_refs[b // per][level, b % per, t * 8 : t * 8 + 8, at] for t in tiles]
+                s = (jnp.concatenate(adv, axis=1) + above[b]) * par_ref[16 * level + 8 + b]
                 solved.append(s)
                 above[b] = par_ref[b] * s
+            whole = jnp.concatenate(solved, axis=0)
+            coarse = whole.astype(jnp.bfloat16)
+            fine = (whole - coarse.astype(jnp.float32)).astype(jnp.bfloat16)
+            mixed = jnp.dot(
+                mix_ref[...], jnp.concatenate([coarse, coarse, fine], axis=0), preferred_element_type=jnp.float32
+            )
             for i in range(bins):
-                loss = loss_ref[i * bins] * solved[0]
-                for j in range(1, bins):
-                    loss = loss + loss_ref[i * bins + j] * solved[j]
                 total = solved[i]
-                base = i * bins * bins
                 for j in range(bins):
-                    inner = gain_ref[base + j * bins] * solved[0]
-                    for k in range(1, j + 1):
-                        inner = inner + gain_ref[base + j * bins + k] * solved[k]
-                    total = total + inner * solved[j]
-                out_ref[level, i, row, at] = total / (1.0 + loss)
+                    row = 8 * (bins + i * bins + j)
+                    total = total + mixed[row : row + 8] * solved[j]
+                total = total / (1.0 + mixed[8 * i : 8 * i + 8])
+                for t in tiles:
+                    out_ref[level, i, t * 8 : t * 8 + 8, at] = total[:, t * LANES : (t + 1) * LANES]
         return carry
 
-    lax.fori_loop(0, (lats // 8) * parts, part, 0)
-
-
-def finish(params, loss, gain, adv, h):
+    lax.fori_loop(0, lons // LANES, part, 0, unroll=True)
+
+
+def mixing(coag_loss, coag_gain):
+    bins = coag_loss.shape[0]
+    both = jnp.concatenate([coag_loss, coag_gain.reshape(bins * bins, bins)], axis=0)
+    eye = jnp.eye(8, dtype=jnp.float32)
+    matrix = (both[:, None, :, None] * eye[None, :, None, :]).reshape(both.shape[0] * 8, bins * 8)
+    coarse = matrix.astype(jnp.bfloat16)
+    fine = (matrix - coarse.astype(jnp.float32)).astype(jnp.bfloat16)
+    return jnp.concatenate([coarse, fine, coarse], axis=1)
+
+
+def finish(params, mix, adv, h):
     levels, per, lats, lons = adv[0].shape
     bins = per * HALVES
     rows = ROWS // 2
@@ -402,14 +412,14 @@
         finish_kernel,
         out_shape=jax.ShapeDtypeStruct((levels, bins, lats, lons), jnp.float32),
         grid=(lats // rows,),
-        in_specs=[SMEM] * 3
+        in_specs=[SMEM, VMEM]
         + [pl.BlockSpec((levels, per, rows, lons), lambda step: (0, 0, step, 0))] * HALVES
         + [pl.BlockSpec((rows // 8, per, 8, lons), lambda step: (step, 0, 0, 0))] * HALVES,
         out_specs=pl.BlockSpec((levels, bins, rows, lons), lambda step: (0, 0, step, 0)),
         compiler_params=BIG,
-        cost_estimate=cost(18),
+        cost_estimate=cost(10),
         name="finish",
-    )(params, loss, gain, *adv, *h)
+    )(params, mix, *adv, *h)
 
 
 def shifted(value, axis, steps):
@@ -428,10 +438,10 @@
 
     per = bins // HALVES
     early_rim = shifted(field[-1, :per], "lev", 1)
+    slots = route(parcel_mass, parcel_owner, parcel_cell, devices, lats * lons)
+    slots, courant = lax.optimization_barrier((slots, courant))
     courant_next = shifted(courant[2, 0], "lev", -1)
     courant_halo = shifted(courant[:, :, -8:], "lat", 1)
-
-    slots = route(parcel_mass, parcel_owner, parcel_cell, devices, lats * lons)
     slots = lax.all_to_all(slots, ("lat", "lev"), split_axis=0, concat_axis=0, tiled=True)
     cap_lanes = slots.shape[2] - LANES
     blocks = cap_lanes // LANES
@@ -456,8 +466,7 @@
     params = lax.dynamic_index_in_dim(table, here, axis=2, keepdims=False).reshape(4 * bins)
     lam = (table[0] * table[1] * table[2] * table[3]).T
     lam = lax.dynamic_slice_in_dim(lam, here // cube * cube, cube, axis=0)
-    gain = coag_gain + jnp.swapaxes(coag_gain, 1, 2)
-    gain = jnp.where(jnp.eye(bins, dtype=bool)[None], coag_gain, gain)
+    mix = mixing(coag_loss, coag_gain)
 
     groups = [list(range(c * cube, (c + 1) * cube)) for c in range(cubes)]
     swap = functools.partial(
@@ -476,7 +485,7 @@
         hs.append(swap(hl))
     for half in range(HALVES):
         hs[half] = swap(carry_scan(hs[half], lam[:, half * per : (half + 1) * per], cubes))
-    return finish(params, coag_loss.reshape(-1), gain.reshape(-1), advs, hs)
+    return finish(params, mix, advs, hs)
 
 
 def carry_scan(hl, lam, cubes):

time: 209 us -> 192 us (0.919)
  waiting for transfers between devices: 45.5 us -> 35.8 us
  Pallas kernels: 79.9 us -> 70.5 us
  starting transfers between devices: 61.8 us -> 65.1 us
  local copies, waits for them, and re-layouts: 14.4 us -> 11.9 us
    pallas_call x1, Pallas kernels: 20.7 us -> 9.2 us  [finish(): pl.pallas_call(finish_kernel, out_shape=jax.ShapeDtypeStruct((levels, bin...]
    ppermute x9, waiting for transfers between devices: 27.4 us -> 21.5 us  [shifted(): lax.ppermute(value, axis, [(source, source + steps) for source in range(f...]
    all_to_all x1, waiting for transfers between devices: 4.28 us -> 1.06 us  [on_device(): lax.all_to_all(slots, ('lat', 'lev'), split_axis=0, concat_axis=0, tiled=...]
    unnamed x28 -> x26, local copies, waits for them, and re-layouts: 5.1 us -> 3.06 us
  transfers between devices with their start and end apart: 14 -> 14, of which waited for: 8 -> 8; matrix products, arithmetic and copies ran while one was open for 7% -> 9% of each run, Pallas kernels for 28% -> 30%
where the time goes in v2:
time: 192 us; the launch traced here: 191 us
  Pallas kernels  70.5 us (37%)
  starting transfers between devices  65.1 us (34%)
  waiting for transfers between devices  35.8 us (19%)
  local copies, waits for them, and re-layouts  11.9 us (6%)
  other arithmetic  7.3 us (4%)
    ppermute x9, starting transfers between devices, shifted(): lax.ppermute(value, axis, [(source, source + steps) for source in range(f...  30.1 us
    pallas_call x2, Pallas kernels, deposit(): pl.pallas_call(functools.partial(deposit_kernel, bool(fields)), out_shape...  28.6 us
    ppermute x9, waiting for transfers between devices, shifted(): lax.ppermute(value, axis, [(source, source + steps) for source in range(f...  21.5 us
    pallas_call x2, Pallas kernels, advance(): pl.pallas_call(functools.partial(advance_kernel, half * bins), out_shape=...  19.7 us
    all_to_all x2, starting transfers between devices, on_device(): hs.append(swap(hl))  19.1 us
    all_to_all x2, waiting for transfers between devices, on_device(): swap(carry_scan(hs[half], lam[:, half * per:(half + 1) * per], cubes))  11.8 us
    pallas_call x1, Pallas kernels, finish(): pl.pallas_call(finish_kernel, out_shape=jax.ShapeDtypeStruct((levels, bin...  9.2 us
    all_to_all x2, starting transfers between devices, on_device(): swap(carry_scan(hs[half], lam[:, half * per:(half + 1) * per], cubes))  8.62 us
  transfers between devices with their start and end apart: 14, of which 8 were waited for; matrix products, arithmetic and copies ran while one was open for 9% of the time, Pallas kernels for 30%

profile of v2, /device:TPU:0, one launch (start us, length us, event | category | flops | bytes accessed | tf_op | source)
XLA Modules:
  0.0 190.9 jit_solution(6825636763999515652)
XLA Ops:
  0.0 4.0 %route.1 = f32[32,8,384]{2,1,0:T(8,128)} custom-call(s32[1,4096]{1,0:T(1,128)} %bitcast.55, s32[1,4096]{1,0:T(1,128)} %bitcast.56, f32[8,4096]{1,0:T(8,128)} %mass_ref.1), custom_call_target="tpu_custom_call" | custom-call | flops 4400000000 | bytes 14400000 | tf_op jit(solution)/shard_map/route/pallas_call | solution.py:93
  4.0 7.3 %all-to-all-start = ((f32[32,8,384]{2,1,0:T(8,128)}), f32[32,8,384]{2,1,0:T(8,128)S(1)}, u32[]{:S(2)}, u32[]{:S(2)}) async-start(f32[32,8,384]{2,1,0:T(8,128)} %route.1), calls=%async_computation | async-start | bytes 786432 | tf_op jit(solution)/shard_map/all_to_all | solution.py:445
  11.3 1.8 slice_bitcast_fusion
  13.1 4.7 %collective-permute-start = (f32[4,64,1152]{2,1,0:T(8,128)S(1)}, f32[4,64,1152]{2,1,0:T(8,128)}, u32[]{:S(2)}, u32[]{:S(2)}) collective-permute-start(f32[4,64,1152]{2,1,0:T(8,128)S(1)} %get-tuple-element.28), channel_id=1, source_target_pairs={{0,1},{1,2},{2,3},{3,4},{4,5},{5,6},{6,7},{7,8},{8,9},{9,10},{10,1... | collective-permute-start | bytes 3538952 | tf_op jit(solution)/shard_map/ppermute | solution.py:428
  17.8 1.0 slice_bitcast_fusion.2
  18.8 1.3 collective-permute-start.4
  20.1 1.6 slice.65
  21.7 2.5 %collective-permute-start.3 = (f32[3,2,8,1152]{3,2,1,0:T(8,128)}, f32[3,2,8,1152]{3,2,1,0:T(8,128)}, u32[]{:S(2)}, u32[]{:S(2)}) collective-permute-start(f32[3,2,8,1152]{3,2,1,0:T(8,128)} %slice.65), channel_id=1, source_target_pairs={{0,16},{1,17},{2,18},{3,19},{4,20},{5,21},{6,22},{7,23},{8,24},{9,... | collective-permute-start | bytes 663560 | tf_op jit(solution)/shard_map/ppermute | solution.py:428
  24.2 0.1 copy.32
  24.3 1.1 all-to-all-done.slots_ref
  25.3 0.7 add_select_fusion.1.rows_ref
  26.0 3.2 %collective-permute-start.1 = (f32[32,8,384]{2,1,0:T(8,128)S(1)}, f32[32,8,384]{2,1,0:T(8,128)S(1)}, u32[]{:S(2)}, u32[]{:S(2)}) collective-permute-start(f32[32,8,384]{2,1,0:T(8,128)S(1)} %all-to-all-done.slots_ref), channel_id=1, source_target_pairs={{0,1},{1,2},{2,3},{3,4},{4,5},{5,6},{6,7},{7,8},{8,9},{9,10},{10,1... | collective-permute-start | bytes 1179656 | tf_op jit(solution)/shard_map/ppermute | solution.py:428
  29.3 1.2 fusion.6.counts_ref
  30.5 23.5 %deposit.1.f_ref = f32[2,8,64,1152]{3,2,1,0:T(8,128)} custom-call(s32[8192]{0:T(1024)} %add_select_fusion.1.rows_ref, s32[32]{0:T(128)} %fusion.6.counts_ref, f32[32,8,384]{2,1,0:T(8,128)} %copy-done.3, f32[2,8,64,1152]{3,2,1,0:T(8,128)} %refs_0_.1), custom_call_target="tpu_custom_call" | custom-call | flops 24199999488 | bytes 79200000 | tf_op jit(solution)/shard_map/deposit/pallas_call | solution.py:215
  54.0 1.1 fusion.12
  55.1 3.6 %collective-permute-done.1.slots_ref = f32[32,8,384]{2,1,0:T(8,128)S(1)} collective-permute-done((f32[32,8,384]{2,1,0:T(8,128)S(1)}, f32[32,8,384]{2,1,0:T(8,128)S(1)}, u32[]{:S(2)}, u32[]{:S(2)}) %collective-permute-start.1) | collective-permute-done | bytes 393248 | tf_op jit(solution)/shard_map/ppermute | solution.py:428
  58.7 1.2 convert_reduce_fusion.counts_ref
  59.9 0.6 add_select_fusion.2.rows_ref
  60.5 5.5 %collective-permute-start.5 = (f32[4,64,1152]{2,1,0:T(8,128)S(1)}, f32[4,64,1152]{2,1,0:T(8,128)}, u32[]{:S(2)}, u32[]{:S(2)}) collective-permute-start(f32[4,64,1152]{2,1,0:T(8,128)S(1)} %get-tuple-element.19), channel_id=1, source_target_pairs={{0,1},{1,2},{2,3},{3,4},{4,5},{5,6},{6,7},{7,8},{8,9},{9,10},{10,1... | collective-permute-start | bytes 3538952 | tf_op jit(solution)/shard_map/ppermute | solution.py:428
  66.0 5.1 %deposit_rim.1 = f32[1,8,64,1152]{3,2,1,0:T(8,128)} custom-call(s32[8192]{0:T(1024)} %add_select_fusion.2.rows_ref, s32[32]{0:T(128)} %convert_reduce_fusion.counts_ref, f32[32,8,384]{2,1,0:T(8,128)} %copy-done.5), custom_call_target="tpu_custom_call" | custom-call | flops 13200000000 | bytes 43200000 | tf_op jit(solution)/shard_map/deposit_rim/pallas_call | solution.py:215
  71.2 1.0 fusion.1
  72.2 1.3 collective-permute-start.2
  73.5 0.1 copy.33
  73.6 0.1 copy.34
  73.7 0.2 fusion.7
  73.8 0.7 reshape.70.par_ref
  74.5 0.4 collective-permute-done.2.halo_ref
  74.9 0.8 copy-done.8
  75.7 9.8 %advance.2 = (f32[2,4,64,1152]{3,2,1,0:T(8,128)}, f32[8,4,8,1152]{3,2,1,0:T(8,128)}) custom-call(f32[32]{0:T(128)} %reshape.70.par_ref, f32[2,8,64,1152]{3,2,1,0:T(8,128)} %deposit.1.f_ref, f32[4,64,1152]{2,1,0:T(8,128)} %collective-permute-done.rim_ref, f32[8,64,1152]{2,1,0:T(8,128)} %bitcast.51, f32[3,4,8,1152]{3,2,1,0:T(8,128)} %copy-done.8, ...), custom_call_target="tpu_custom_call" | custom-call | flops 9900000256 | bytes 32400000 | tf_op jit(solution)/shard_map/advance/pallas_call | solution.py:306
  85.5 15.3 %all-to-all-start.1 = ((f32[8,4,8,1152]{3,2,1,0:T(8,128)}), f32[8,4,8,1152]{3,2,1,0:T(8,128)S(1)}, u32[]{:S(2)}, u32[]{:S(2)}) async-start(f32[8,4,8,1152]{3,2,1,0:T(8,128)} %get-tuple-element.23), calls=%async_computation.1 | async-start | bytes 2359296 | tf_op jit(solution)/shard_map/all_to_all | solution.py:485
  100.8 1.0 fusion
  101.8 2.0 %collective-permute-start.6 = (f32[3,4,8,1152]{3,2,1,0:T(8,128)S(1)}, f32[3,4,8,1152]{3,2,1,0:T(8,128)S(1)}, u32[]{:S(2)}, u32[]{:S(2)}) collective-permute-start(f32[3,4,8,1152]{3,2,1,0:T(8,128)S(1)} %pad_maximum_fusion.1), channel_id=1, source_target_pairs={{0,16},{1,17},{2,18},{3,19},{4,20},{5,21},{6,22},{7,23},{8,24},{9,... | collective-permute-start | bytes 1327112 | tf_op jit(solution)/shard_map/ppermute | solution.py:428
  103.9 1.4 collective-permute-done.6.halo_ref
  105.2 0.8 copy-done.9
  106.0 9.8 %advance.3 = (f32[2,4,64,1152]{3,2,1,0:T(8,128)}, f32[8,4,8,1152]{3,2,1,0:T(8,128)}) custom-call(f32[32]{0:T(128)} %reshape.70.par_ref, f32[2,8,64,1152]{3,2,1,0:T(8,128)} %deposit.1.f_ref, f32[4,64,1152]{2,1,0:T(8,128)} %collective-permute-done.5.rim_ref, f32[8,64,1152]{2,1,0:T(8,128)} %bitcast.53, f32[3,4,8,1152]{3,2,1,0:T(8,128)} %copy-done.9, ...), custom_call_target="tpu_custom_call" | custom-call | flops 9900000256 | bytes 32400000 | tf_op jit(solution)/shard_map/advance/pallas_call | solution.py:306
  115.8 1.5 all-to-all-done.1.hl_ref
  117.3 3.8 %all-to-all-start.3 = ((f32[8,4,8,1152]{3,2,1,0:T(8,128)}), f32[8,4,8,1152]{3,2,1,0:T(8,128)S(1)}, u32[]{:S(2)}, u32[]{:S(2)}) async-start(f32[8,4,8,1152]{3,2,1,0:T(8,128)} %get-tuple-element.24), calls=%async_computation.3 | async-start | bytes 2359296 | tf_op jit(solution)/shard_map/all_to_all | solution.py:485
  121.1 0.1 dynamic-slice_bitcast_fusion
  121.2 0.1 copy.43
  121.3 0.7 reshape.76.lam_ref
  121.9 2.1 %cube_end.2 = f32[4,8,1152]{2,1,0:T(8,128)} custom-call(f32[32]{0:T(128)} %reshape.76.lam_ref, f32[8,4,8,1152]{3,2,1,0:T(8,128)} %copy-done), custom_call_target="tpu_custom_call" | custom-call | flops 2200000000 | bytes 7200000 | tf_op jit(solution)/shard_map/cube_end/pallas_call | solution.py:494
  124.0 4.4 %collective-permute-start.7 = (f32[4,8,1152]{2,1,0:T(8,128)}, f32[4,8,1152]{2,1,0:T(8,128)S(1)}, u32[]{:S(2)}, u32[]{:S(2)}) collective-permute-start(f32[4,8,1152]{2,1,0:T(8,128)} %cube_end.2), channel_id=1, source_target_pairs={{0,8},{1,9},{2,10},{3,11},{4,12},{5,13},{6,14},{7,15},{16,24},{17,... | collective-permute-start | bytes 442376 | tf_op jit(solution)/shard_map/ppermute | solution.py:428
  128.4 8.9 %collective-permute-done.7.hin_ref = f32[4,8,1152]{2,1,0:T(8,128)S(1)} collective-permute-done((f32[4,8,1152]{2,1,0:T(8,128)}, f32[4,8,1152]{2,1,0:T(8,128)S(1)}, u32[]{:S(2)}, u32[]{:S(2)}) %collective-permute-start.7) | collective-permute-done | bytes 147488 | tf_op jit(solution)/shard_map/ppermute | solution.py:428
  137.4 0.7 copy-done.10
  138.0 2.4 %cube_scan.2 = f32[8,4,8,1152]{3,2,1,0:T(8,128)} custom-call(f32[32]{0:T(128)} %reshape.76.lam_ref, f32[8,4,8,1152]{3,2,1,0:T(8,128)} %copy-done, f32[4,8,1152]{2,1,0:T(8,128)} %copy-done.10), custom_call_target="tpu_custom_call" | custom-call | flops 2200000000 | bytes 7200000 | tf_op jit(solution)/shard_map/cube_scan/pallas_call | solution.py:510
  140.5 4.2 %all-to-all-start.2 = ((f32[8,4,8,1152]{3,2,1,0:T(8,128)}), f32[8,4,8,1152]{3,2,1,0:T(8,128)S(1)}, u32[]{:S(2)}, u32[]{:S(2)}) async-start(f32[8,4,8,1152]{3,2,1,0:T(8,128)} %cube_scan.2), calls=%async_computation.2 | async-start | bytes 2359296 | tf_op jit(solution)/shard_map/all_to_all | solution.py:487
  144.6 0.1 copy.44
  144.7 0.6 reshape.77.lam_ref
  145.3 2.1 %cube_end.3 = f32[4,8,1152]{2,1,0:T(8,128)} custom-call(f32[32]{0:T(128)} %reshape.77.lam_ref, f32[8,4,8,1152]{3,2,1,0:T(8,128)} %copy-done.1), custom_call_target="tpu_custom_call" | custom-call | flops 2200000000 | bytes 7200000 | tf_op jit(solution)/shard_map/cube_end/pallas_call | solution.py:494
  147.4 5.2 %collective-permute-start.8 = (f32[4,8,1152]{2,1,0:T(8,128)}, f32[4,8,1152]{2,1,0:T(8,128)S(1)}, u32[]{:S(2)}, u32[]{:S(2)}) collective-permute-start(f32[4,8,1152]{2,1,0:T(8,128)} %cube_end.3), channel_id=1, source_target_pairs={{0,8},{1,9},{2,10},{3,11},{4,12},{5,13},{6,14},{7,15},{16,24},{17,... | collective-permute-start | bytes 442376 | tf_op jit(solution)/shard_map/ppermute | solution.py:428
  152.6 7.3 %collective-permute-done.8.hin_ref = f32[4,8,1152]{2,1,0:T(8,128)S(1)} collective-permute-done((f32[4,8,1152]{2,1,0:T(8,128)}, f32[4,8,1152]{2,1,0:T(8,128)S(1)}, u32[]{:S(2)}, u32[]{:S(2)}) %collective-permute-start.8) | collective-permute-done | bytes 147488 | tf_op jit(solution)/shard_map/ppermute | solution.py:428
  159.8 0.7 copy-done.11
  160.5 2.5 %cube_scan.3 = f32[8,4,8,1152]{3,2,1,0:T(8,128)} custom-call(f32[32]{0:T(128)} %reshape.77.lam_ref, f32[8,4,8,1152]{3,2,1,0:T(8,128)} %copy-done.1, f32[4,8,1152]{2,1,0:T(8,128)} %copy-done.11), custom_call_target="tpu_custom_call" | custom-call | flops 2200000000 | bytes 7200000 | tf_op jit(solution)/shard_map/cube_scan/pallas_call | solution.py:510
  163.0 4.5 %all-to-all-start.4 = ((f32[8,4,8,1152]{3,2,1,0:T(8,128)}), f32[8,4,8,1152]{3,2,1,0:T(8,128)}, u32[]{:S(2)}, u32[]{:S(2)}) async-start(f32[8,4,8,1152]{3,2,1,0:T(8,128)} %cube_scan.3), calls=%async_computation.4 | async-start | bytes 2359296 | tf_op jit(solution)/shard_map/all_to_all | solution.py:487
  167.5 0.1 copy.36
  167.6 0.1 copy.45
  167.6 0.1 pad_maximum_fusion.3
  167.7 0.2 broadcast_multiply_fusion
  167.9 0.7 mul.32
  168.6 0.1 copy.38
  168.8 0.1 copy.39
  169.0 0.9 pad_maximum_fusion.2.mix_ref
  169.9 11.8 %all-to-all-done.4.refs_3_ = f32[8,4,8,1152]{3,2,1,0:T(8,128)} async-done(((f32[8,4,8,1152]{3,2,1,0:T(8,128)}), f32[8,4,8,1152]{3,2,1,0:T(8,128)}, u32[]{:S(2)}, u32[]{:S(2)}) %all-to-all-start.4) | async-done | bytes 1179680 | tf_op jit(solution)/shard_map/all_to_all | solution.py:487
  181.7 9.2 %finish.1 = f32[2,8,64,1152]{3,2,1,0:T(8,128)} custom-call(f32[32]{0:T(128)} %reshape.70.par_ref, bf16[576,192]{1,0:T(8,128)(2,1)} %pad_maximum_fusion.2.mix_ref, f32[2,4,64,1152]{3,2,1,0:T(8,128)} %get-tuple-element.20.refs_0_, f32[2,4,64,1152]{3,2,1,0:T(8,128)} %get-tuple-element.22.refs_1_, f32[8,4,8,1152]{3,2,1,0:T(8,128)} %copy-done.2, ...), custom_call_target="tpu_custom_call" | custom-call | flops 11000000512 | bytes 36000000 | tf_op jit(solution)/shard_map/finish/pallas_call | solution.py:411
  (37 shorter events, 0.2 us)
Async XLA Ops:
  4.0 21.3 %all-to-all-start = ((f32[32,8,384]{2,1,0:T(8,128)}), f32[32,8,384]{2,1,0:T(8,128)S(1)}, u32[]{:S(2)}, u32[]{:S(2)}) async-start(f32[32,8,384]{2,1,0:T(8,128)} %route.1), calls=%async_computation | async-start | bytes 786432 | tf_op jit(solution)/shard_map/all_to_all | solution.py:445
  11.3 12.9 %copy-start.6 = (f32[8,32]{1,0:T(8,128)S(1)}, f32[8,32]{1,0:T(8,128)}, u32[]{:S(2)}) copy-start(f32[8,32]{1,0:T(8,128)} %param.13) | copy-start | bytes 3076
  13.1 58.0 %collective-permute-start = (f32[4,64,1152]{2,1,0:T(8,128)S(1)}, f32[4,64,1152]{2,1,0:T(8,128)}, u32[]{:S(2)}, u32[]{:S(2)}) collective-permute-start(f32[4,64,1152]{2,1,0:T(8,128)S(1)} %get-tuple-element.28), channel_id=1, source_target_pairs={{0,1},{1,2},{2,3},{3,4},{4,5},{5,6},{6,7},{7,8},{8,9},{9,10},{10,1... | collective-permute-start | bytes 3538952 | tf_op jit(solution)/shard_map/ppermute | solution.py:428
  18.8 55.7 %collective-permute-start.4 = (f32[64,1152]{1,0:T(8,128)S(1)}, f32[64,1152]{1,0:T(8,128)}, u32[]{:S(2)}, u32[]{:S(2)}) collective-permute-start(f32[64,1152]{1,0:T(8,128)S(1)} %slice_bitcast_fusion.2), channel_id=1, source_target_pairs={{1,0},{2,1},{3,2},{4,3},{5,4},{6,5},{7,6},{8,7},{9,8},{10,9},{11,1... | collective-permute-start | bytes 884744 | tf_op jit(solution)/shard_map/ppermute | solution.py:428
  21.7 52.8 %collective-permute-start.3 = (f32[3,2,8,1152]{3,2,1,0:T(8,128)}, f32[3,2,8,1152]{3,2,1,0:T(8,128)}, u32[]{:S(2)}, u32[]{:S(2)}) collective-permute-start(f32[3,2,8,1152]{3,2,1,0:T(8,128)} %slice.65), channel_id=1, source_target_pairs={{0,16},{1,17},{2,18},{3,19},{4,20},{5,21},{6,22},{7,23},{8,24},{9,... | collective-permute-start | bytes 663560 | tf_op jit(solution)/shard_map/ppermute | solution.py:428
  25.3 5.2 %copy-start.3 = (f32[32,8,384]{2,1,0:T(8,128)}, f32[32,8,384]{2,1,0:T(8,128)S(1)}, u32[]{:S(2)}) copy-start(f32[32,8,384]{2,1,0:T(8,128)S(1)} %all-to-all-done.slots_ref) | copy-start | bytes 1179652
  26.0 32.6 %collective-permute-start.1 = (f32[32,8,384]{2,1,0:T(8,128)S(1)}, f32[32,8,384]{2,1,0:T(8,128)S(1)}, u32[]{:S(2)}, u32[]{:S(2)}) collective-permute-start(f32[32,8,384]{2,1,0:T(8,128)S(1)} %all-to-all-done.slots_ref), channel_id=1, source_target_pairs={{0,1},{1,2},{2,3},{3,4},{4,5},{5,6},{6,7},{7,8},{8,9},{9,10},{10,1... | collective-permute-start | bytes 1179656 | tf_op jit(solution)/shard_map/ppermute | solution.py:428
  58.6 7.4 %copy-start.5 = (f32[32,8,384]{2,1,0:T(8,128)}, f32[32,8,384]{2,1,0:T(8,128)S(1)}, u32[]{:S(2)}) copy-start(f32[32,8,384]{2,1,0:T(8,128)S(1)} %collective-permute-done.1.slots_ref) | copy-start | bytes 1179652
  60.5 40.3 %collective-permute-start.5 = (f32[4,64,1152]{2,1,0:T(8,128)S(1)}, f32[4,64,1152]{2,1,0:T(8,128)}, u32[]{:S(2)}, u32[]{:S(2)}) collective-permute-start(f32[4,64,1152]{2,1,0:T(8,128)S(1)} %get-tuple-element.19), channel_id=1, source_target_pairs={{0,1},{1,2},{2,3},{3,4},{4,5},{5,6},{6,7},{7,8},{8,9},{9,10},{10,1... | collective-permute-start | bytes 3538952 | tf_op jit(solution)/shard_map/ppermute | solution.py:428
  72.2 2.7 %collective-permute-start.2 = (f32[3,4,8,1152]{3,2,1,0:T(8,128)S(1)}, f32[3,4,8,1152]{3,2,1,0:T(8,128)S(1)}, u32[]{:S(2)}, u32[]{:S(2)}) collective-permute-start(f32[3,4,8,1152]{3,2,1,0:T(8,128)S(1)} %pad_maximum_fusion), channel_id=1, source_target_pairs={{0,16},{1,17},{2,18},{3,19},{4,20},{5,21},{6,22},{7,23},{8,24},{9,... | collective-permute-start | bytes 1327112 | tf_op jit(solution)/shard_map/ppermute | solution.py:428
  74.9 0.8 copy-start.8
  85.5 31.8 %all-to-all-start.1 = ((f32[8,4,8,1152]{3,2,1,0:T(8,128)}), f32[8,4,8,1152]{3,2,1,0:T(8,128)S(1)}, u32[]{:S(2)}, u32[]{:S(2)}) async-start(f32[8,4,8,1152]{3,2,1,0:T(8,128)} %get-tuple-element.23), calls=%async_computation.1 | async-start | bytes 2359296 | tf_op jit(solution)/shard_map/all_to_all | solution.py:485
  101.8 3.4 %collective-permute-start.6 = (f32[3,4,8,1152]{3,2,1,0:T(8,128)S(1)}, f32[3,4,8,1152]{3,2,1,0:T(8,128)S(1)}, u32[]{:S(2)}, u32[]{:S(2)}) collective-permute-start(f32[3,4,8,1152]{3,2,1,0:T(8,128)S(1)} %pad_maximum_fusion.1), channel_id=1, source_target_pairs={{0,16},{1,17},{2,18},{3,19},{4,20},{5,21},{6,22},{7,23},{8,24},{9,... | collective-permute-start | bytes 1327112 | tf_op jit(solution)/shard_map/ppermute | solution.py:428
  105.2 0.8 copy-start.9
  117.3 4.6 %copy-start = (f32[8,4,8,1152]{3,2,1,0:T(8,128)}, f32[8,4,8,1152]{3,2,1,0:T(8,128)S(1)}, u32[]{:S(2)}) copy-start(f32[8,4,8,1152]{3,2,1,0:T(8,128)S(1)} %all-to-all-done.1.hl_ref) | copy-start | bytes 3538948
  117.3 23.2 %all-to-all-start.3 = ((f32[8,4,8,1152]{3,2,1,0:T(8,128)}), f32[8,4,8,1152]{3,2,1,0:T(8,128)S(1)}, u32[]{:S(2)}, u32[]{:S(2)}) async-start(f32[8,4,8,1152]{3,2,1,0:T(8,128)} %get-tuple-element.24), calls=%async_computation.3 | async-start | bytes 2359296 | tf_op jit(solution)/shard_map/all_to_all | solution.py:485
  124.0 13.4 %collective-permute-start.7 = (f32[4,8,1152]{2,1,0:T(8,128)}, f32[4,8,1152]{2,1,0:T(8,128)S(1)}, u32[]{:S(2)}, u32[]{:S(2)}) collective-permute-start(f32[4,8,1152]{2,1,0:T(8,128)} %cube_end.2), channel_id=1, source_target_pairs={{0,8},{1,9},{2,10},{3,11},{4,12},{5,13},{6,14},{7,15},{16,24},{17,... | collective-permute-start | bytes 442376 | tf_op jit(solution)/shard_map/ppermute | solution.py:428
  137.4 0.7 copy-start.10
  140.5 4.8 %copy-start.1 = (f32[8,4,8,1152]{3,2,1,0:T(8,128)}, f32[8,4,8,1152]{3,2,1,0:T(8,128)S(1)}, u32[]{:S(2)}) copy-start(f32[8,4,8,1152]{3,2,1,0:T(8,128)S(1)} %all-to-all-done.3.hl_ref) | copy-start | bytes 3538948
  140.5 22.5 %all-to-all-start.2 = ((f32[8,4,8,1152]{3,2,1,0:T(8,128)}), f32[8,4,8,1152]{3,2,1,0:T(8,128)S(1)}, u32[]{:S(2)}, u32[]{:S(2)}) async-start(f32[8,4,8,1152]{3,2,1,0:T(8,128)} %cube_scan.2), calls=%async_computation.2 | async-start | bytes 2359296 | tf_op jit(solution)/shard_map/all_to_all | solution.py:487
  147.4 12.5 %collective-permute-start.8 = (f32[4,8,1152]{2,1,0:T(8,128)}, f32[4,8,1152]{2,1,0:T(8,128)S(1)}, u32[]{:S(2)}, u32[]{:S(2)}) collective-permute-start(f32[4,8,1152]{2,1,0:T(8,128)} %cube_end.3), channel_id=1, source_target_pairs={{0,8},{1,9},{2,10},{3,11},{4,12},{5,13},{6,14},{7,15},{16,24},{17,... | collective-permute-start | bytes 442376 | tf_op jit(solution)/shard_map/ppermute | solution.py:428
  159.8 0.7 copy-start.11
  163.0 4.5 %copy-start.7 = (f32[8,8]{1,0:T(8,128)S(1)}, f32[8,8]{1,0:T(8,128)}, u32[]{:S(2)}) copy-start(f32[8,8]{1,0:T(8,128)} %param.15) | copy-start | bytes 772
  163.0 4.6 %copy-start.4 = (f32[8,8,8]{2,1,0:T(8,128)S(1)}, f32[8,8,8]{2,1,0:T(8,128)}, u32[]{:S(2)}) copy-start(f32[8,8,8]{2,1,0:T(8,128)} %param.14) | copy-start | bytes 6148
  163.0 4.6 %copy-start.2 = (f32[8,4,8,1152]{3,2,1,0:T(8,128)}, f32[8,4,8,1152]{3,2,1,0:T(8,128)S(1)}, u32[]{:S(2)}) copy-start(f32[8,4,8,1152]{3,2,1,0:T(8,128)S(1)} %all-to-all-done.2.refs_2_) | copy-start | bytes 3538948
  163.0 18.7 %all-to-all-start.4 = ((f32[8,4,8,1152]{3,2,1,0:T(8,128)}), f32[8,4,8,1152]{3,2,1,0:T(8,128)}, u32[]{:S(2)}, u32[]{:S(2)}) async-start(f32[8,4,8,1152]{3,2,1,0:T(8,128)} %cube_scan.3), calls=%async_computation.4 | async-start | bytes 2359296 | tf_op jit(solution)/shard_map/all_to_all | solution.py:487

commit v3 on v2

--- a/solution.py
+++ b/solution.py
@@ -12,6 +12,7 @@
 ROUTE_BLOCK = 256
 ACCS = 4
 ROWS = 32
+MERGE_ROWS = 64
 HALVES = 2
 VMEM = pl.BlockSpec(memory_space=pltpu.VMEM)
 SMEM = pl.BlockSpec(memory_space=pltpu.SMEM)
@@ -106,13 +107,13 @@
     )(parcel_owner.reshape(1, parcels), parcel_cell.reshape(1, parcels), parcel_mass)
 
 
-def deposit_kernel(with_field, rows_ref, counts_ref, slots_ref, *refs):
+def deposit_kernel(with_field, item, rows_ref, counts_ref, slots_ref, *refs):
     if with_field:
         field_ref, *refs = refs
     out_ref, list_ref, pick_ref, even_ref, odd_ref, *accs = refs
     sources, unused, width = slots_ref.shape
     cap_lanes = width - LANES
-    blocks = cap_lanes // LANES
+    pieces = cap_lanes // item
     unused, bins, lats, lons = out_ref.shape
     lon_blocks = lons // LANES
     rows = accs[0].shape[0] - 8
@@ -135,9 +136,9 @@
         tile_row = lax.broadcasted_iota(jnp.int32, (8, LANES), 0)
 
         def note(source, active):
-            for block in range(blocks):
-                list_ref[active] = source * blocks + block
-                active = active + jnp.where(counts_ref[source] > block * LANES, 1, 0)
+            for piece in range(pieces):
+                list_ref[active] = source * pieces + piece
+                active = active + jnp.where(counts_ref[source] > piece * item, 1, 0)
             return active
 
         active = lax.fori_loop(0, sources, note, 0)
@@ -145,9 +146,11 @@
             list_ref[active + extra] = 0
 
         def spread(index, spread_ref):
-            item = list_ref[index]
-            source = item // blocks
-            block = item % blocks
+            entry = list_ref[index]
+            source = entry // pieces
+            piece = entry % pieces
+            block = piece * item // LANES
+            picked = pl.ds(pl.multiple_of(piece % (LANES // item) * (8 * item), 8 * item), 8 * item)
             live = jnp.where(index < active, 1.0, 0.0)
             mass = slots_ref[source, :, pl.ds(pl.multiple_of(block * LANES, LANES), LANES)] * live
             code = slots_ref[source, :, pl.ds(cap_lanes, LANES)]
@@ -155,7 +158,7 @@
             hot = jnp.where(lane_ids == (code & (LANES - 1)), 1.0, 0.0).astype(jnp.bfloat16)
             coarse = mass.astype(jnp.bfloat16).astype(jnp.float32)
             parts = [
-                pick_ref[...] * jnp.tile(jnp.concatenate([part, part], axis=0).astype(jnp.bfloat16), (LANES // 2, 1))
+                pick_ref[picked] * jnp.tile(jnp.concatenate([part, part], axis=0).astype(jnp.bfloat16), (item // 2, 1))
                 for part in (coarse, mass - coarse)
             ]
             spread_ref[...] = lax.dot_general(
@@ -166,8 +169,8 @@
             )
 
         def add(index, spread_ref):
-            base = list_ref[index] * LANES
-            for first in range(0, LANES, ACCS):
+            base = list_ref[index] * item
+            for first in range(0, item, ACCS):
                 places = [rows_ref[base + first + k] for k in range(ACCS)]
                 held = [acc[place] for acc, place in zip(accs, places)]
                 for k in range(ACCS):
@@ -201,28 +204,28 @@
                     out_ref[0, b, pl.ds(lat, 8), at] = total
 
 
-def deposit(field, shape, slots, cell_rows, counts, name):
+def deposit(field, shape, slots, cell_rows, counts, item, name):
     levels, bins, lats, lons = shape
     rows = levels * lats * lons // LANES
-    per = lats // ROWS
+    per = lats // MERGE_ROWS
 
     def at(step):
         block = jnp.maximum(step - 1, 0)
         return (block // per, 0, block % per, 0)
 
-    spec = pl.BlockSpec((1, bins, ROWS, lons), at)
+    spec = pl.BlockSpec((1, bins, MERGE_ROWS, lons), at)
     fields = [] if field is None else [field]
     return pl.pallas_call(
-        functools.partial(deposit_kernel, bool(fields)),
+        functools.partial(deposit_kernel, bool(fields), item),
         out_shape=jax.ShapeDtypeStruct(shape, jnp.float32),
         grid=(1 + levels * per,),
         in_specs=[SMEM, SMEM, VMEM] + [spec] * len(fields),
         out_specs=spec,
         scratch_shapes=[
-            pltpu.SMEM((cell_rows.shape[0] // LANES + 8,), jnp.int32),
+            pltpu.SMEM((cell_rows.shape[0] // item + 8,), jnp.int32),
             pltpu.VMEM((8 * LANES, LANES), jnp.bfloat16),
-            pltpu.VMEM((8 * LANES, LANES), jnp.float32),
-            pltpu.VMEM((8 * LANES, LANES), jnp.float32),
+            pltpu.VMEM((8 * item, LANES), jnp.float32),
+            pltpu.VMEM((8 * item, LANES), jnp.float32),
         ]
         + [pltpu.VMEM((rows + 8, 8, LANES), jnp.float32)] * ACCS,
         compiler_params=BIG,
@@ -454,12 +457,12 @@
         return codes // LANES, counts
 
     rows, counts = tables(slots, blocks)
-    f0 = deposit(field, field.shape, slots, rows, counts, "deposit")
+    f0 = deposit(field, field.shape, slots, rows, counts, LANES, "deposit")
     rim_slots, later_rim = lax.optimization_barrier((rim_slots, field[-1, per:]))
     raw_rims = [early_rim, shifted(later_rim, "lev", 1)]
     rows, counts = tables(rim_slots, blocks + 1)
     rows = jnp.where(rows < level_rows, level_rows, rows - level_rows)
-    drop = deposit(None, (1,) + field.shape[1:], rim_slots, rows, counts, "deposit_rim")[0]
+    drop = deposit(None, (1,) + field.shape[1:], rim_slots, rows, counts, LANES // 2, "deposit_rim")[0]
     pairs = settle.reshape(bins, n_lev, 2)
     first, second = pairs[:, :, 0], pairs[:, :, 1]
     table = jnp.stack([first, 1.0 / (1.0 + first), second, 1.0 / (1.0 + second)], axis=0)

time: 192 us -> 193 us (level)
  transfers between devices with their start and end apart: 14 -> 14, of which waited for: 8 -> 8; matrix products, arithmetic and copies ran while one was open for 9% -> 9% of each run, Pallas kernels for 30% -> 31%
where the time goes in v3:
time: 193 us; the launch traced here: 191 us
  Pallas kernels  71.8 us (37%)
  starting transfers between devices  66 us (34%)
  waiting for transfers between devices  34.1 us (18%)
  local copies, waits for them, and re-layouts  11.9 us (6%)
  other arithmetic  7.3 us (4%)
    ppermute x9, starting transfers between devices, shifted(): lax.ppermute(value, axis, [(source, source + steps) for source in range(f...  30.7 us
    pallas_call x2, Pallas kernels, deposit(): pl.pallas_call(functools.partial(deposit_kernel, bool(fields), item), out...  29.9 us
    ppermute x9, waiting for transfers between devices, shifted(): lax.ppermute(value, axis, [(source, source + steps) for source in range(f...  19.8 us
    pallas_call x2, Pallas kernels, advance(): pl.pallas_call(functools.partial(advance_kernel, half * bins), out_shape=...  19.7 us
    all_to_all x2, starting transfers between devices, on_device(): hs.append(swap(hl))  19.6 us
    all_to_all x2, waiting for transfers between devices, on_device(): swap(carry_scan(hs[half], lam[:, half * per:(half + 1) * per], cubes))  11.8 us
    pallas_call x1, Pallas kernels, finish(): pl.pallas_call(finish_kernel, out_shape=jax.ShapeDtypeStruct((levels, bin...  9.2 us
    all_to_all x2, starting transfers between devices, on_device(): swap(carry_scan(hs[half], lam[:, half * per:(half + 1) * per], cubes))  8.37 us
  transfers between devices with their start and end apart: 14, of which 8 were waited for; matrix products, arithmetic and copies ran while one was open for 9% of the time, Pallas kernels for 31%

profile of v3, /device:TPU:0, one launch (start us, length us, event | category | flops | bytes accessed | tf_op | source)
XLA Modules:
  0.0 191.4 jit_solution(6275366729534421724)
XLA Ops:
  0.0 4.0 %route.1 = f32[32,8,384]{2,1,0:T(8,128)} custom-call(s32[1,4096]{1,0:T(1,128)} %bitcast.55, s32[1,4096]{1,0:T(1,128)} %bitcast.56, f32[8,4096]{1,0:T(8,128)} %mass_ref.1), custom_call_target="tpu_custom_call" | custom-call | flops 4400000000 | bytes 14400000 | tf_op jit(solution)/shard_map/route/pallas_call | solution.py:94
  4.0 7.3 %all-to-all-start = ((f32[32,8,384]{2,1,0:T(8,128)}), f32[32,8,384]{2,1,0:T(8,128)S(1)}, u32[]{:S(2)}, u32[]{:S(2)}) async-start(f32[32,8,384]{2,1,0:T(8,128)} %route.1), calls=%async_computation | async-start | bytes 786432 | tf_op jit(solution)/shard_map/all_to_all | solution.py:448
  11.3 1.8 slice_bitcast_fusion
  13.1 4.7 %collective-permute-start = (f32[4,64,1152]{2,1,0:T(8,128)S(1)}, f32[4,64,1152]{2,1,0:T(8,128)}, u32[]{:S(2)}, u32[]{:S(2)}) collective-permute-start(f32[4,64,1152]{2,1,0:T(8,128)S(1)} %get-tuple-element.28), channel_id=1, source_target_pairs={{0,1},{1,2},{2,3},{3,4},{4,5},{5,6},{6,7},{7,8},{8,9},{9,10},{10,1... | collective-permute-start | bytes 3538952 | tf_op jit(solution)/shard_map/ppermute | solution.py:431
  17.8 1.0 slice_bitcast_fusion.2
  18.8 1.3 collective-permute-start.4
  20.1 1.6 slice.65
  21.7 2.5 %collective-permute-start.3 = (f32[3,2,8,1152]{3,2,1,0:T(8,128)}, f32[3,2,8,1152]{3,2,1,0:T(8,128)}, u32[]{:S(2)}, u32[]{:S(2)}) collective-permute-start(f32[3,2,8,1152]{3,2,1,0:T(8,128)} %slice.65), channel_id=1, source_target_pairs={{0,16},{1,17},{2,18},{3,19},{4,20},{5,21},{6,22},{7,23},{8,24},{9,... | collective-permute-start | bytes 663560 | tf_op jit(solution)/shard_map/ppermute | solution.py:431
  24.2 0.1 copy.32
  24.3 1.1 all-to-all-done.slots_ref
  25.3 0.7 add_select_fusion.1.rows_ref
  26.0 3.2 %collective-permute-start.1 = (f32[32,8,384]{2,1,0:T(8,128)S(1)}, f32[32,8,384]{2,1,0:T(8,128)S(1)}, u32[]{:S(2)}, u32[]{:S(2)}) collective-permute-start(f32[32,8,384]{2,1,0:T(8,128)S(1)} %all-to-all-done.slots_ref), channel_id=1, source_target_pairs={{0,1},{1,2},{2,3},{3,4},{4,5},{5,6},{6,7},{7,8},{8,9},{9,10},{10,1... | collective-permute-start | bytes 1179656 | tf_op jit(solution)/shard_map/ppermute | solution.py:431
  29.3 1.2 fusion.6.counts_ref
  30.5 24.4 %deposit.1.f_ref = f32[2,8,64,1152]{3,2,1,0:T(8,128)} custom-call(s32[8192]{0:T(1024)} %add_select_fusion.1.rows_ref, s32[32]{0:T(128)} %fusion.6.counts_ref, f32[32,8,384]{2,1,0:T(8,128)} %copy-done.3, f32[2,8,64,1152]{3,2,1,0:T(8,128)} %refs_0_.1), custom_call_target="tpu_custom_call" | custom-call | flops 24199999488 | bytes 79200000 | tf_op jit(solution)/shard_map/deposit/pallas_call | solution.py:218
  54.9 1.1 fusion.12
  56.0 2.7 %collective-permute-done.1.slots_ref = f32[32,8,384]{2,1,0:T(8,128)S(1)} collective-permute-done((f32[32,8,384]{2,1,0:T(8,128)S(1)}, f32[32,8,384]{2,1,0:T(8,128)S(1)}, u32[]{:S(2)}, u32[]{:S(2)}) %collective-permute-start.1) | collective-permute-done | bytes 393248 | tf_op jit(solution)/shard_map/ppermute | solution.py:431
  58.7 1.2 convert_reduce_fusion.counts_ref
  59.9 0.6 add_select_fusion.2.rows_ref
  60.5 5.5 %collective-permute-start.5 = (f32[4,64,1152]{2,1,0:T(8,128)S(1)}, f32[4,64,1152]{2,1,0:T(8,128)}, u32[]{:S(2)}, u32[]{:S(2)}) collective-permute-start(f32[4,64,1152]{2,1,0:T(8,128)S(1)} %get-tuple-element.19), channel_id=1, source_target_pairs={{0,1},{1,2},{2,3},{3,4},{4,5},{5,6},{6,7},{7,8},{8,9},{9,10},{10,1... | collective-permute-start | bytes 3538952 | tf_op jit(solution)/shard_map/ppermute | solution.py:431
  66.0 5.5 %deposit_rim.1 = f32[1,8,64,1152]{3,2,1,0:T(8,128)} custom-call(s32[8192]{0:T(1024)} %add_select_fusion.2.rows_ref, s32[32]{0:T(128)} %convert_reduce_fusion.counts_ref, f32[32,8,384]{2,1,0:T(8,128)} %copy-done.5), custom_call_target="tpu_custom_call" | custom-call | flops 13200000000 | bytes 43200000 | tf_op jit(solution)/shard_map/deposit_rim/pallas_call | solution.py:218
  71.6 1.0 fusion.1
  72.6 1.3 collective-permute-start.2
  73.9 0.1 copy.33
  74.0 0.1 copy.34
  74.1 0.2 fusion.7
  74.3 0.7 reshape.70.par_ref
  74.9 0.4 collective-permute-done.2.halo_ref
  75.3 0.8 copy-done.8
  76.1 9.8 %advance.2 = (f32[2,4,64,1152]{3,2,1,0:T(8,128)}, f32[8,4,8,1152]{3,2,1,0:T(8,128)}) custom-call(f32[32]{0:T(128)} %reshape.70.par_ref, f32[2,8,64,1152]{3,2,1,0:T(8,128)} %deposit.1.f_ref, f32[4,64,1152]{2,1,0:T(8,128)} %collective-permute-done.rim_ref, f32[8,64,1152]{2,1,0:T(8,128)} %bitcast.51, f32[3,4,8,1152]{3,2,1,0:T(8,128)} %copy-done.8, ...), custom_call_target="tpu_custom_call" | custom-call | flops 9900000256 | bytes 32400000 | tf_op jit(solution)/shard_map/advance/pallas_call | solution.py:309
  85.9 15.2 %all-to-all-start.1 = ((f32[8,4,8,1152]{3,2,1,0:T(8,128)}), f32[8,4,8,1152]{3,2,1,0:T(8,128)S(1)}, u32[]{:S(2)}, u32[]{:S(2)}) async-start(f32[8,4,8,1152]{3,2,1,0:T(8,128)} %get-tuple-element.23), calls=%async_computation.1 | async-start | bytes 2359296 | tf_op jit(solution)/shard_map/all_to_all | solution.py:488
  101.1 1.0 fusion
  102.2 2.0 %collective-permute-start.6 = (f32[3,4,8,1152]{3,2,1,0:T(8,128)S(1)}, f32[3,4,8,1152]{3,2,1,0:T(8,128)S(1)}, u32[]{:S(2)}, u32[]{:S(2)}) collective-permute-start(f32[3,4,8,1152]{3,2,1,0:T(8,128)S(1)} %pad_maximum_fusion.1), channel_id=1, source_target_pairs={{0,16},{1,17},{2,18},{3,19},{4,20},{5,21},{6,22},{7,23},{8,24},{9,... | collective-permute-start | bytes 1327112 | tf_op jit(solution)/shard_map/ppermute | solution.py:431
  104.2 1.4 collective-permute-done.6.halo_ref
  105.6 0.8 copy-done.9
  106.4 9.8 %advance.3 = (f32[2,4,64,1152]{3,2,1,0:T(8,128)}, f32[8,4,8,1152]{3,2,1,0:T(8,128)}) custom-call(f32[32]{0:T(128)} %reshape.70.par_ref, f32[2,8,64,1152]{3,2,1,0:T(8,128)} %deposit.1.f_ref, f32[4,64,1152]{2,1,0:T(8,128)} %collective-permute-done.5.rim_ref, f32[8,64,1152]{2,1,0:T(8,128)} %bitcast.53, f32[3,4,8,1152]{3,2,1,0:T(8,128)} %copy-done.9, ...), custom_call_target="tpu_custom_call" | custom-call | flops 9900000256 | bytes 32400000 | tf_op jit(solution)/shard_map/advance/pallas_call | solution.py:309
  116.2 1.5 all-to-all-done.1.hl_ref
  117.6 4.4 %all-to-all-start.3 = ((f32[8,4,8,1152]{3,2,1,0:T(8,128)}), f32[8,4,8,1152]{3,2,1,0:T(8,128)S(1)}, u32[]{:S(2)}, u32[]{:S(2)}) async-start(f32[8,4,8,1152]{3,2,1,0:T(8,128)} %get-tuple-element.24), calls=%async_computation.3 | async-start | bytes 2359296 | tf_op jit(solution)/shard_map/all_to_all | solution.py:488
  122.0 0.1 dynamic-slice_bitcast_fusion
  122.1 0.1 copy.43
  122.2 0.7 reshape.76.lam_ref
  122.9 2.1 %cube_end.2 = f32[4,8,1152]{2,1,0:T(8,128)} custom-call(f32[32]{0:T(128)} %reshape.76.lam_ref, f32[8,4,8,1152]{3,2,1,0:T(8,128)} %copy-done), custom_call_target="tpu_custom_call" | custom-call | flops 2200000000 | bytes 7200000 | tf_op jit(solution)/shard_map/cube_end/pallas_call | solution.py:497
  124.9 5.1 %collective-permute-start.7 = (f32[4,8,1152]{2,1,0:T(8,128)}, f32[4,8,1152]{2,1,0:T(8,128)S(1)}, u32[]{:S(2)}, u32[]{:S(2)}) collective-permute-start(f32[4,8,1152]{2,1,0:T(8,128)} %cube_end.2), channel_id=1, source_target_pairs={{0,8},{1,9},{2,10},{3,11},{4,12},{5,13},{6,14},{7,15},{16,24},{17,... | collective-permute-start | bytes 442376 | tf_op jit(solution)/shard_map/ppermute | solution.py:431
  130.0 8.1 %collective-permute-done.7.hin_ref = f32[4,8,1152]{2,1,0:T(8,128)S(1)} collective-permute-done((f32[4,8,1152]{2,1,0:T(8,128)}, f32[4,8,1152]{2,1,0:T(8,128)S(1)}, u32[]{:S(2)}, u32[]{:S(2)}) %collective-permute-start.7) | collective-permute-done | bytes 147488 | tf_op jit(solution)/shard_map/ppermute | solution.py:431
  138.1 0.7 copy-done.10
  138.7 2.4 %cube_scan.2 = f32[8,4,8,1152]{3,2,1,0:T(8,128)} custom-call(f32[32]{0:T(128)} %reshape.76.lam_ref, f32[8,4,8,1152]{3,2,1,0:T(8,128)} %copy-done, f32[4,8,1152]{2,1,0:T(8,128)} %copy-done.10), custom_call_target="tpu_custom_call" | custom-call | flops 2200000000 | bytes 7200000 | tf_op jit(solution)/shard_map/cube_scan/pallas_call | solution.py:513
  141.2 3.9 %all-to-all-start.2 = ((f32[8,4,8,1152]{3,2,1,0:T(8,128)}), f32[8,4,8,1152]{3,2,1,0:T(8,128)S(1)}, u32[]{:S(2)}, u32[]{:S(2)}) async-start(f32[8,4,8,1152]{3,2,1,0:T(8,128)} %cube_scan.2), calls=%async_computation.2 | async-start | bytes 2359296 | tf_op jit(solution)/shard_map/all_to_all | solution.py:490
  145.1 0.1 copy.44
  145.2 0.6 reshape.77.lam_ref
  145.8 2.1 %cube_end.3 = f32[4,8,1152]{2,1,0:T(8,128)} custom-call(f32[32]{0:T(128)} %reshape.77.lam_ref, f32[8,4,8,1152]{3,2,1,0:T(8,128)} %copy-done.1), custom_call_target="tpu_custom_call" | custom-call | flops 2200000000 | bytes 7200000 | tf_op jit(solution)/shard_map/cube_end/pallas_call | solution.py:497
  147.8 5.2 %collective-permute-start.8 = (f32[4,8,1152]{2,1,0:T(8,128)}, f32[4,8,1152]{2,1,0:T(8,128)S(1)}, u32[]{:S(2)}, u32[]{:S(2)}) collective-permute-start(f32[4,8,1152]{2,1,0:T(8,128)} %cube_end.3), channel_id=1, source_target_pairs={{0,8},{1,9},{2,10},{3,11},{4,12},{5,13},{6,14},{7,15},{16,24},{17,... | collective-permute-start | bytes 442376 | tf_op jit(solution)/shard_map/ppermute | solution.py:431
  153.0 7.3 %collective-permute-done.8.hin_ref = f32[4,8,1152]{2,1,0:T(8,128)S(1)} collective-permute-done((f32[4,8,1152]{2,1,0:T(8,128)}, f32[4,8,1152]{2,1,0:T(8,128)S(1)}, u32[]{:S(2)}, u32[]{:S(2)}) %collective-permute-start.8) | collective-permute-done | bytes 147488 | tf_op jit(solution)/shard_map/ppermute | solution.py:431
  160.3 0.7 copy-done.11
  161.0 2.5 %cube_scan.3 = f32[8,4,8,1152]{3,2,1,0:T(8,128)} custom-call(f32[32]{0:T(128)} %reshape.77.lam_ref, f32[8,4,8,1152]{3,2,1,0:T(8,128)} %copy-done.1, f32[4,8,1152]{2,1,0:T(8,128)} %copy-done.11), custom_call_target="tpu_custom_call" | custom-call | flops 2200000000 | bytes 7200000 | tf_op jit(solution)/shard_map/cube_scan/pallas_call | solution.py:513
  163.5 4.5 %all-to-all-start.4 = ((f32[8,4,8,1152]{3,2,1,0:T(8,128)}), f32[8,4,8,1152]{3,2,1,0:T(8,128)}, u32[]{:S(2)}, u32[]{:S(2)}) async-start(f32[8,4,8,1152]{3,2,1,0:T(8,128)} %cube_scan.3), calls=%async_computation.4 | async-start | bytes 2359296 | tf_op jit(solution)/shard_map/all_to_all | solution.py:490
  167.9 0.1 copy.36
  168.0 0.1 copy.45
  168.1 0.1 pad_maximum_fusion.3
  168.2 0.2 broadcast_multiply_fusion
  168.4 0.7 mul.32
  169.1 0.1 copy.38
  169.2 0.1 copy.39
  169.4 0.9 pad_maximum_fusion.2.mix_ref
  170.3 11.8 %all-to-all-done.4.refs_3_ = f32[8,4,8,1152]{3,2,1,0:T(8,128)} async-done(((f32[8,4,8,1152]{3,2,1,0:T(8,128)}), f32[8,4,8,1152]{3,2,1,0:T(8,128)}, u32[]{:S(2)}, u32[]{:S(2)}) %all-to-all-start.4) | async-done | bytes 1179680 | tf_op jit(solution)/shard_map/all_to_all | solution.py:490
  182.2 9.2 %finish.1 = f32[2,8,64,1152]{3,2,1,0:T(8,128)} custom-call(f32[32]{0:T(128)} %reshape.70.par_ref, bf16[576,192]{1,0:T(8,128)(2,1)} %pad_maximum_fusion.2.mix_ref, f32[2,4,64,1152]{3,2,1,0:T(8,128)} %get-tuple-element.20.refs_0_, f32[2,4,64,1152]{3,2,1,0:T(8,128)} %get-tuple-element.22.refs_1_, f32[8,4,8,1152]{3,2,1,0:T(8,128)} %copy-done.2, ...), custom_call_target="tpu_custom_call" | custom-call | flops 11000000512 | bytes 36000000 | tf_op jit(solution)/shard_map/finish/pallas_call | solution.py:414
  (37 shorter events, 0.2 us)
Async XLA Ops:
  4.0 21.3 %all-to-all-start = ((f32[32,8,384]{2,1,0:T(8,128)}), f32[32,8,384]{2,1,0:T(8,128)S(1)}, u32[]{:S(2)}, u32[]{:S(2)}) async-start(f32[32,8,384]{2,1,0:T(8,128)} %route.1), calls=%async_computation | async-start | bytes 786432 | tf_op jit(solution)/shard_map/all_to_all | solution.py:448
  11.3 12.9 %copy-start.6 = (f32[8,32]{1,0:T(8,128)S(1)}, f32[8,32]{1,0:T(8,128)}, u32[]{:S(2)}) copy-start(f32[8,32]{1,0:T(8,128)} %param.13) | copy-start | bytes 3076
  13.1 58.4 %collective-permute-start = (f32[4,64,1152]{2,1,0:T(8,128)S(1)}, f32[4,64,1152]{2,1,0:T(8,128)}, u32[]{:S(2)}, u32[]{:S(2)}) collective-permute-start(f32[4,64,1152]{2,1,0:T(8,128)S(1)} %get-tuple-element.28), channel_id=1, source_target_pairs={{0,1},{1,2},{2,3},{3,4},{4,5},{5,6},{6,7},{7,8},{8,9},{9,10},{10,1... | collective-permute-start | bytes 3538952 | tf_op jit(solution)/shard_map/ppermute | solution.py:431
  18.8 56.1 %collective-permute-start.4 = (f32[64,1152]{1,0:T(8,128)S(1)}, f32[64,1152]{1,0:T(8,128)}, u32[]{:S(2)}, u32[]{:S(2)}) collective-permute-start(f32[64,1152]{1,0:T(8,128)S(1)} %slice_bitcast_fusion.2), channel_id=1, source_target_pairs={{1,0},{2,1},{3,2},{4,3},{5,4},{6,5},{7,6},{8,7},{9,8},{10,9},{11,1... | collective-permute-start | bytes 884744 | tf_op jit(solution)/shard_map/ppermute | solution.py:431
  21.7 53.2 %collective-permute-start.3 = (f32[3,2,8,1152]{3,2,1,0:T(8,128)}, f32[3,2,8,1152]{3,2,1,0:T(8,128)}, u32[]{:S(2)}, u32[]{:S(2)}) collective-permute-start(f32[3,2,8,1152]{3,2,1,0:T(8,128)} %slice.65), channel_id=1, source_target_pairs={{0,16},{1,17},{2,18},{3,19},{4,20},{5,21},{6,22},{7,23},{8,24},{9,... | collective-permute-start | bytes 663560 | tf_op jit(solution)/shard_map/ppermute | solution.py:431
  25.3 5.2 %copy-start.3 = (f32[32,8,384]{2,1,0:T(8,128)}, f32[32,8,384]{2,1,0:T(8,128)S(1)}, u32[]{:S(2)}) copy-start(f32[32,8,384]{2,1,0:T(8,128)S(1)} %all-to-all-done.slots_ref) | copy-start | bytes 1179652
  26.0 32.6 %collective-permute-start.1 = (f32[32,8,384]{2,1,0:T(8,128)S(1)}, f32[32,8,384]{2,1,0:T(8,128)S(1)}, u32[]{:S(2)}, u32[]{:S(2)}) collective-permute-start(f32[32,8,384]{2,1,0:T(8,128)S(1)} %all-to-all-done.slots_ref), channel_id=1, source_target_pairs={{0,1},{1,2},{2,3},{3,4},{4,5},{5,6},{6,7},{7,8},{8,9},{9,10},{10,1... | collective-permute-start | bytes 1179656 | tf_op jit(solution)/shard_map/ppermute | solution.py:431
  58.6 7.4 %copy-start.5 = (f32[32,8,384]{2,1,0:T(8,128)}, f32[32,8,384]{2,1,0:T(8,128)S(1)}, u32[]{:S(2)}) copy-start(f32[32,8,384]{2,1,0:T(8,128)S(1)} %collective-permute-done.1.slots_ref) | copy-start | bytes 1179652
  60.5 40.6 %collective-permute-start.5 = (f32[4,64,1152]{2,1,0:T(8,128)S(1)}, f32[4,64,1152]{2,1,0:T(8,128)}, u32[]{:S(2)}, u32[]{:S(2)}) collective-permute-start(f32[4,64,1152]{2,1,0:T(8,128)S(1)} %get-tuple-element.19), channel_id=1, source_target_pairs={{0,1},{1,2},{2,3},{3,4},{4,5},{5,6},{6,7},{7,8},{8,9},{9,10},{10,1... | collective-permute-start | bytes 3538952 | tf_op jit(solution)/shard_map/ppermute | solution.py:431
  72.6 2.7 %collective-permute-start.2 = (f32[3,4,8,1152]{3,2,1,0:T(8,128)S(1)}, f32[3,4,8,1152]{3,2,1,0:T(8,128)S(1)}, u32[]{:S(2)}, u32[]{:S(2)}) collective-permute-start(f32[3,4,8,1152]{3,2,1,0:T(8,128)S(1)} %pad_maximum_fusion), channel_id=1, source_target_pairs={{0,16},{1,17},{2,18},{3,19},{4,20},{5,21},{6,22},{7,23},{8,24},{9,... | collective-permute-start | bytes 1327112 | tf_op jit(solution)/shard_map/ppermute | solution.py:431
  75.3 0.8 copy-start.8
  85.9 31.7 %all-to-all-start.1 = ((f32[8,4,8,1152]{3,2,1,0:T(8,128)}), f32[8,4,8,1152]{3,2,1,0:T(8,128)S(1)}, u32[]{:S(2)}, u32[]{:S(2)}) async-start(f32[8,4,8,1152]{3,2,1,0:T(8,128)} %get-tuple-element.23), calls=%async_computation.1 | async-start | bytes 2359296 | tf_op jit(solution)/shard_map/all_to_all | solution.py:488
  102.2 3.4 %collective-permute-start.6 = (f32[3,4,8,1152]{3,2,1,0:T(8,128)S(1)}, f32[3,4,8,1152]{3,2,1,0:T(8,128)S(1)}, u32[]{:S(2)}, u32[]{:S(2)}) collective-permute-start(f32[3,4,8,1152]{3,2,1,0:T(8,128)S(1)} %pad_maximum_fusion.1), channel_id=1, source_target_pairs={{0,16},{1,17},{2,18},{3,19},{4,20},{5,21},{6,22},{7,23},{8,24},{9,... | collective-permute-start | bytes 1327112 | tf_op jit(solution)/shard_map/ppermute | solution.py:431
  105.6 0.8 copy-start.9
  117.6 5.2 %copy-start = (f32[8,4,8,1152]{3,2,1,0:T(8,128)}, f32[8,4,8,1152]{3,2,1,0:T(8,128)S(1)}, u32[]{:S(2)}) copy-start(f32[8,4,8,1152]{3,2,1,0:T(8,128)S(1)} %all-to-all-done.1.hl_ref) | copy-start | bytes 3538948
  117.6 23.5 %all-to-all-start.3 = ((f32[8,4,8,1152]{3,2,1,0:T(8,128)}), f32[8,4,8,1152]{3,2,1,0:T(8,128)S(1)}, u32[]{:S(2)}, u32[]{:S(2)}) async-start(f32[8,4,8,1152]{3,2,1,0:T(8,128)} %get-tuple-element.24), calls=%async_computation.3 | async-start | bytes 2359296 | tf_op jit(solution)/shard_map/all_to_all | solution.py:488
  124.9 13.1 %collective-permute-start.7 = (f32[4,8,1152]{2,1,0:T(8,128)}, f32[4,8,1152]{2,1,0:T(8,128)S(1)}, u32[]{:S(2)}, u32[]{:S(2)}) collective-permute-start(f32[4,8,1152]{2,1,0:T(8,128)} %cube_end.2), channel_id=1, source_target_pairs={{0,8},{1,9},{2,10},{3,11},{4,12},{5,13},{6,14},{7,15},{16,24},{17,... | collective-permute-start | bytes 442376 | tf_op jit(solution)/shard_map/ppermute | solution.py:431
  138.1 0.7 copy-start.10
  141.2 4.6 %copy-start.1 = (f32[8,4,8,1152]{3,2,1,0:T(8,128)}, f32[8,4,8,1152]{3,2,1,0:T(8,128)S(1)}, u32[]{:S(2)}) copy-start(f32[8,4,8,1152]{3,2,1,0:T(8,128)S(1)} %all-to-all-done.3.hl_ref) | copy-start | bytes 3538948
  141.2 22.3 %all-to-all-start.2 = ((f32[8,4,8,1152]{3,2,1,0:T(8,128)}), f32[8,4,8,1152]{3,2,1,0:T(8,128)S(1)}, u32[]{:S(2)}, u32[]{:S(2)}) async-start(f32[8,4,8,1152]{3,2,1,0:T(8,128)} %cube_scan.2), calls=%async_computation.2 | async-start | bytes 2359296 | tf_op jit(solution)/shard_map/all_to_all | solution.py:490
  147.8 12.5 %collective-permute-start.8 = (f32[4,8,1152]{2,1,0:T(8,128)}, f32[4,8,1152]{2,1,0:T(8,128)S(1)}, u32[]{:S(2)}, u32[]{:S(2)}) collective-permute-start(f32[4,8,1152]{2,1,0:T(8,128)} %cube_end.3), channel_id=1, source_target_pairs={{0,8},{1,9},{2,10},{3,11},{4,12},{5,13},{6,14},{7,15},{16,24},{17,... | collective-permute-start | bytes 442376 | tf_op jit(solution)/shard_map/ppermute | solution.py:431
  160.3 0.7 copy-start.11
  163.5 4.5 %copy-start.7 = (f32[8,8]{1,0:T(8,128)S(1)}, f32[8,8]{1,0:T(8,128)}, u32[]{:S(2)}) copy-start(f32[8,8]{1,0:T(8,128)} %param.15) | copy-start | bytes 772
  163.5 4.6 %copy-start.4 = (f32[8,8,8]{2,1,0:T(8,128)S(1)}, f32[8,8,8]{2,1,0:T(8,128)}, u32[]{:S(2)}) copy-start(f32[8,8,8]{2,1,0:T(8,128)} %param.14) | copy-start | bytes 6148
  163.5 4.6 %copy-start.2 = (f32[8,4,8,1152]{3,2,1,0:T(8,128)}, f32[8,4,8,1152]{3,2,1,0:T(8,128)S(1)}, u32[]{:S(2)}) copy-start(f32[8,4,8,1152]{3,2,1,0:T(8,128)S(1)} %all-to-all-done.2.refs_2_) | copy-start | bytes 3538948
  163.5 18.7 %all-to-all-start.4 = ((f32[8,4,8,1152]{3,2,1,0:T(8,128)}), f32[8,4,8,1152]{3,2,1,0:T(8,128)}, u32[]{:S(2)}, u32[]{:S(2)}) async-start(f32[8,4,8,1152]{3,2,1,0:T(8,128)} %cube_scan.3), calls=%async_computation.4 | async-start | bytes 2359296 | tf_op jit(solution)/shard_map/all_to_all | solution.py:490
